TPU v7x, 512 devices: a whole 4x4x16 slice. The times are simulated.
512 devices in a mesh: dp: 64 (over y_lo, z, core), fsdp: 8 (over y_hi, x).
Axes of the slice: x: 4, y: 4 (y_hi: 2, y_lo: 2; y = y_hi * 2 + y_lo), z: 16, core: 2. Of those that a mesh axis runs over, the one named last changes fastest.
Arguments:
- acts: bfloat16 [65536, 2048], P(('dp', 'fsdp')), may hold values from -6 to 6
- grad_out: bfloat16 [65536, 2048], P(('dp', 'fsdp')), may hold values from -60 to 60
- weight: bfloat16 [2048, 2048], P('fsdp'), may hold values from -0.125 to 0.125
- basis: bfloat16 [2048, 512], P('fsdp'), may hold values from -3 to 3
- first_moment: float32 [512, 2048], P(('dp', 'fsdp')), may hold values from -4 to 4
- second_moment: float32 [512, 2048], P(('dp', 'fsdp')), may hold values from 0.0001 to 0.01
Outputs:
- grad_in: bfloat16 [65536, 2048], P(('dp', 'fsdp'))
- first_new: float32 [512, 2048], P(('dp', 'fsdp'))
- second_new: float32 [512, 2048], P(('dp', 'fsdp'))
- weight_update: bfloat16 [2048, 2048], P('fsdp')
All inputs are finite; a program needn't handle non-finite values.
Results may differ from a plain program's by a relative error of at most 0.0056.
Values may be sent and summed in bfloat16 or wider, within the bound.
No kernel may reach another device: no remote copies, remote signals or barrier semaphores. Data moves between devices by JAX's collectives and lax.ppermute only.
A program may use at most 64 MiB of HBM per device.

v0:
```python
import math

import jax
import jax.numpy as jnp
from jax import lax
from jax.sharding import PartitionSpec as P

D_OUT = 2048
RANK = 512


first_bias = 1.0 - 0.9**10
second_bias = 1.0 - 0.999**10


def on_device(acts, grad_out, weight, basis, first_moment, second_moment):
    contract_last = (((1,), (1,)), ((), ()))
    grad_in = lax.dot_general(
        grad_out,
        lax.all_gather(weight, "fsdp", axis=0, tiled=True),
        contract_last,
        preferred_element_type=jnp.float32,
    ).astype(jnp.bfloat16)
    columns = acts
    coords = jnp.dot(
        columns,
        lax.all_gather(basis, "fsdp", axis=0, tiled=True),
        preferred_element_type=jnp.float32,
    ).astype(jnp.bfloat16)
    projected = lax.psum_scatter(
        lax.dot_general(
            coords, grad_out, (((0,), (0,)), ((), ())), preferred_element_type=jnp.float32
        ),
        ("dp", "fsdp"),
        scatter_dimension=0,
        tiled=True,
    )
    total = lax.psum(jnp.sum(projected * projected), ("dp", "fsdp"))
    limit = math.sqrt(RANK * D_OUT)
    factor = jnp.minimum(1.0, limit / (jnp.sqrt(total) + 1e-06))
    clipped = factor * projected
    first_new = 0.9 * first_moment + 0.1 * clipped
    second_new = 0.999 * second_moment + 0.001 * clipped * clipped
    direction = (first_new / first_bias / (jnp.sqrt(second_new / second_bias) + 1e-08)).astype(
        jnp.bfloat16
    )
    columns = basis
    update = jnp.dot(
        columns,
        lax.all_gather(direction, ("dp", "fsdp"), axis=0, tiled=True),
        preferred_element_type=jnp.float32,
    )
    weight_update = (0.25 * update).astype(jnp.bfloat16)
    return (grad_in, first_new, second_new, weight_update)


def solution(mesh):
    in_specs = (
        P(("dp", "fsdp"), None),
        P(("dp", "fsdp"), None),
        P("fsdp", None),
        P("fsdp", None),
        P(("dp", "fsdp"), None),
        P(("dp", "fsdp"), None),
    )
    out_specs = (
        P(("dp", "fsdp"), None),
        P(("dp", "fsdp"), None),
        P(("dp", "fsdp"), None),
        P("fsdp", None),
    )
    return jax.shard_map(
        on_device, mesh=mesh, in_specs=in_specs, out_specs=out_specs, check_vma=False
    )
```

profile of v0, /device:TPU:1, one launch (start us, length us, event | category | flops | bytes accessed | tf_op | source)
XLA Modules:
  0.0 2211.1 jit_solution(12610434120060992297)
XLA Ops:
  7.2 0.0 copy-start
  7.2 0.0 all-gather.7.cloned.1.call-start
  7.2 0.7 all-gather.7.cloned.1.call-update
  7.9 0.0 copy-start.2
  7.9 0.0 copy-start.3
  7.9 0.0 all-reduce.3.cloned.1.call-start
  8.0 77.6 %all-gather.7.cloned.1.call-done = bf16[2048,512]{1,0:T(8,128)(2,1)} async-done(((bf16[256,512]{1,0:T(8,128)(2,1)}), bf16[2048,512]{1,0:T(8,128)(2,1)}) %all-gather.7.cloned.1.call-update) | async-done | bytes 2097168 | tf_op jit(solution)/shard_map/all_gather | solution.py:27
  85.6 0.0 copy-done
  85.6 4.9 fusion.4
  90.5 0.0 copy-start.1
  90.5 0.0 all-reduce.3.cloned.1.call-update
  90.5 0.0 all-gather.9.cloned.1.call-start
  90.5 488.6 %all-reduce.3.cloned.1.call-done = f32[512,2048]{1,0:T(8,128)} async-done(((f32[512,2048]{1,0:T(8,128)}), f32[512,2048]{1,0:T(8,128)}) %all-reduce.3.cloned.1.call-update) | async-done | bytes 4194320
  579.1 1.5 multiply_reduce_fusion
  580.6 105.6 %psum.7 = f32[]{:T(128)} all-reduce(f32[]{:T(128)} %multiply_reduce_fusion), channel_id=1, replica_groups=mesh['dp'=64,'fsdp'=8] {'dp','fsdp'}, use_global_device_ids=true, to_apply=%region_2.0 | all-reduce | flops 1 | bytes 8 | tf_op jit(solution)/shard_map/psum | solution.py:38
  686.9 0.0 copy-done.2
  686.9 0.0 copy-done.3
  686.9 1.5 convert_bitcast_fusion
  688.4 0.0 all-gather.9.cloned.1.call-update
  688.5 0.0 all-gather.5.cloned.1.call-start
  688.5 0.5 all-gather.5.cloned.1.call-update
  689.0 1381.4 %all-gather.9.cloned.1.call-done = bf16[512,1,2048]{2,1,0:T(2,128)(2,1)} async-done(((bf16[1,1,2048]{2,1,0:T(2,128)(2,1)}), bf16[512,1,2048]{2,1,0:T(2,128)(2,1)}) %all-gather.9.cloned.1.call-update) | async-done | bytes 2097168 | tf_op jit(solution)/shard_map/all_gather | solution.py:50
  2070.4 0.0 copy-done.1
  2070.4 4.5 fusion.1
  2074.9 1.4 copy.12
  2076.3 121.2 %all-gather.5.cloned.1.call-done = bf16[2048,2048]{1,0:T(8,128)(2,1)} async-done(((bf16[256,2048]{1,0:T(8,128)(2,1)}), bf16[2048,2048]{1,0:T(8,128)(2,1)}) %all-gather.5.cloned.1.call-update) | async-done | bytes 8388624 | tf_op jit(solution)/shard_map/all_gather | solution.py:20
  2197.5 7.1 convolution_convert_fusion
Async XLA Ops:
  7.2 78.4 %copy-start = (bf16[128,2048]{1,0:T(8,128)(2,1)S(1)}, bf16[128,2048]{1,0:T(8,128)(2,1)}, u32[]{:S(2)}) copy-start(bf16[128,2048]{1,0:T(8,128)(2,1)} %param.7) | copy-start | bytes 1572868
  7.2 78.4 %all-gather.7.cloned.1.call-start = ((), (), s32[]{:S(2)}) async-start(), calls=%async_computation.1 | async-start | bytes 2359296 | tf_op jit(solution)/shard_map/all_gather | solution.py:27
  7.9 679.0 %copy-start.2 = (f32[1,2048]{1,0:T(1,128)S(1)}, f32[1,2048]{1,0:T(1,128)}, u32[]{:S(2)}) copy-start(f32[1,2048]{1,0:T(1,128)} %param.11) | copy-start | bytes 24580
  7.9 679.0 %copy-start.3 = (f32[1,2048]{1,0:T(1,128)S(1)}, f32[1,2048]{1,0:T(1,128)}, u32[]{:S(2)}) copy-start(f32[1,2048]{1,0:T(1,128)} %param.10) | copy-start | bytes 24580
  7.9 571.2 %all-reduce.3.cloned.1.call-start = ((), (), s32[]{:S(2)}) async-start(), calls=%async_computation.3 | async-start | bytes 8388608
  90.5 1979.9 %copy-start.1 = (bf16[256,512]{1,0:T(8,128)(2,1)S(1)}, bf16[256,512]{1,0:T(8,128)(2,1)}, u32[]{:S(2)}) copy-start(bf16[256,512]{1,0:T(8,128)(2,1)} %param.9) | copy-start | bytes 786436
  90.5 1979.9 %all-gather.9.cloned.1.call-start = ((), (), s32[]{:S(2)}) async-start(), calls=%async_computation.2 | async-start | bytes 4202496 | tf_op jit(solution)/shard_map/all_gather | solution.py:50
  688.5 1509.0 %all-gather.5.cloned.1.call-start = ((), (), s32[]{:S(2)}) async-start(), calls=%async_computation | async-start | bytes 9437184 | tf_op jit(solution)/shard_map/all_gather | solution.py:20
Sparse Core Ops, SparseCore 0:
  11.2 74.3 all-gather.6
  91.0 488.0 all-reduce.2
  688.6 1381.7 all-gather.8
  2073.5 123.9 all-gather.4
where the time goes:
time: 2210 us
  waiting for transfers between devices  2070 us (94%)
  blocking collectives  106 us (5%)
    all_gather x1, waiting for transfers between devices, on_device(): lax.all_gather(direction, ('dp', 'fsdp'), axis=0, tiled=True)  1380 us
    unnamed x5, waiting for transfers between devices  490 us
    all_gather x1, waiting for transfers between devices, on_device(): lax.all_gather(weight, 'fsdp', axis=0, tiled=True)  121 us
    psum x1, blocking collectives, on_device(): total = lax.psum(jnp.sum(projected * projected), ('dp', 'fsdp'))  106 us
    all_gather x1, waiting for transfers between devices, on_device(): lax.all_gather(basis, 'fsdp', axis=0, tiled=True)  77.6 us
  transfers between devices with their start and end apart: 4, of which 4 were waited for; matrix products, arithmetic and copies ran while one was open for 0% of the time, Pallas kernels for 0%

commit v1 on v0

v1 whole, which is shorter than its diff:
```python
import math

import jax
import jax.numpy as jnp
from jax import lax
from jax.sharding import Mesh
from jax.sharding import PartitionSpec as P

D_OUT = 2048
RANK = 512
AXES = ("yl", "z", "c", "yh", "x")
YX = ("yl", "yh", "x")
FSDP = ("yh", "x")
bf16 = jnp.bfloat16
f32 = jnp.float32

first_bias = 1.0 - 0.9**10
second_bias = 1.0 - 0.999**10


def spread(a, axes, peers):
    return lax.all_to_all(
        jnp.broadcast_to(a[None], (peers,) + a.shape), axes, 0, 0, tiled=True
    )


def adam(p, m, v, factor):
    clipped = factor * p
    first_new = 0.9 * m + 0.1 * clipped
    second_new = 0.999 * v + 0.001 * clipped * clipped
    return first_new, second_new


def on_device(acts, grad_out, weight, basis, first_moment, second_moment):
    core = lax.axis_index("c")
    swap = [(0, 1), (1, 0)]

    def other(a):
        return lax.ppermute(a, "c", swap)

    with jax.named_scope("pick"):
        col = lax.broadcasted_iota(jnp.int32, (RANK, RANK), 1)
        row = lax.broadcasted_iota(jnp.int32, (RANK, RANK), 0)
        own = jnp.where(col < 256, core, 1 - core)
        z, x, yh, yl = col % 16, (col // 16) % 4, (col // 64) % 2, (col // 128) % 2
        pick = (row == (((yl * 16 + z) * 2 + own) * 2 + yh) * 4 + x).astype(bf16)
        basis_p = jnp.dot(basis, pick, preferred_element_type=f32).astype(bf16)
    with jax.named_scope("swap_tokens"):
        acts2 = jnp.concatenate([acts, other(acts)], 0)
        grad2 = jnp.concatenate([grad_out, other(grad_out)], 0)
    with jax.named_scope("basis"):
        basis_all = spread(basis_p[:, :256], FSDP, 8).reshape(2048, 256)
    with jax.named_scope("weight"):
        half = lax.dynamic_slice_in_dim(weight, core * 128, 128, 0)
        weight_half = lax.all_gather(half, FSDP, axis=0, tiled=True)
    with jax.named_scope("projected"):
        coords = jnp.dot(acts2, basis_all, preferred_element_type=f32).astype(bf16)
        part = lax.dot_general(
            coords, grad2, (((0,), (0,)), ((), ())), preferred_element_type=f32
        ).astype(bf16)
    with jax.named_scope("sum_yx"):
        part = lax.all_to_all(part.reshape(16, 16, D_OUT), YX, 0, 0, tiled=True)
        part = jnp.sum(part.astype(f32), 0)
    with jax.named_scope("sum_z"):
        part = lax.all_to_all(part.reshape(16, 16, 128), "z", 0, 0, tiled=True)
        p = jnp.sum(part, 0)
    m = first_moment.reshape(16, 128)
    v = second_moment.reshape(16, 128)
    with jax.named_scope("rows_z"):
        rows = spread(jnp.concatenate([p, m, v], 0), "z", 16)
        p16, m16, v16 = rows[:, :16], rows[:, 16:32], rows[:, 32:]
    with jax.named_scope("total"):
        own = jnp.broadcast_to(jnp.sum(p16 * p16), (32, 128))
        sums = lax.all_to_all(own, ("yl", "c", "yh", "x"), 0, 0, tiled=True)
        total = jnp.sum(sums[:, 0])
        limit = math.sqrt(RANK * D_OUT)
        factor = jnp.minimum(1.0, limit / (jnp.sqrt(total) + 1e-06))
    with jax.named_scope("adam"):
        first_new, second_new = adam(p, m, v, factor)
        f16, s16 = adam(p16, m16, v16, factor)
        direction = (f16 / first_bias / (jnp.sqrt(s16 / second_bias) + 1e-08)).astype(bf16)
        direction = direction.reshape(16, D_OUT)
    with jax.named_scope("rows_yx"):
        mine = spread(direction, YX, 16).reshape(256, D_OUT)
    with jax.named_scope("update"):
        theirs = other(mine)
        update = jnp.dot(basis_p[:, :256], mine, preferred_element_type=f32)
        update = update + jnp.dot(basis_p[:, 256:], theirs, preferred_element_type=f32)
        weight_update = (0.25 * update).astype(bf16)
    with jax.named_scope("grad_in"):
        both = lax.dot_general(
            grad2, weight_half, (((1,), (1,)), ((), ())), preferred_element_type=f32
        ).astype(bf16)
        here, there = both[:128], other(both[128:])
        low = jnp.where(core == 0, here, there)
        high = jnp.where(core == 0, there, here)
        parts = []
        for k in range(8):
            parts += [low[:, k * 128 : k * 128 + 128], high[:, k * 128 : k * 128 + 128]]
        grad_in = jnp.concatenate(parts, 1)
    return (
        grad_in,
        first_new.reshape(1, D_OUT),
        second_new.reshape(1, D_OUT),
        weight_update,
    )


def solution(mesh):
    fine = Mesh(mesh.devices.reshape(2, 16, 2, 2, 4), AXES)
    rows = P(AXES, None)
    shared = P(FSDP, None)
    return jax.shard_map(
        on_device,
        mesh=fine,
        in_specs=(rows, rows, shared, shared, rows, rows),
        out_specs=(rows, rows, rows, shared),
        check_vma=False,
    )
```

time: 2210 us -> 176 us (0.08)
  waiting for transfers between devices: 2070 us -> 25.9 us
  starting transfers between devices: 0.16 us -> 24.3 us
    all_gather x3 -> x1, waiting for transfers between devices: 1580 us -> 0.02 us  [on_device(): weight_half = lax.all_gather(half, FSDP, axis=0, tiled=True)]
    unnamed x5 -> x1, waiting for transfers between devices: 490 us -> 0.02 us
    psum x1 -> x0, blocking collectives: 106 us -> none  [on_device(): total = lax.psum(jnp.sum(projected * projected), ('dp', 'fsdp'))]
    all_to_all x0 -> x4, blocking collectives: none -> 87.9 us  [the longest x1 24.6 us: on_device(): part = lax.all_to_all(part.reshape(16, 16, 128), 'z', 0, 0, tiled=True)]
    all_to_all x0 -> x2, waiting for transfers between devices: none -> 25 us  [spread(): lax.all_to_all(jnp.broadcast_to(a[None], (peers,) + a.shape), axes, 0, 0,...]
  transfers between devices with their start and end apart: 4 -> 7, of which waited for: 4 -> 3; matrix products, arithmetic and copies ran while one was open for 0% -> 10% of each run, Pallas kernels for 0% -> 0%
where the time goes in v1:
time: 176 us; the launch traced here: 175 us
  blocking collectives  87.9 us (50%)
  waiting for transfers between devices  25.9 us (15%)
  starting transfers between devices  24.3 us (14%)
  between operations  15.2 us (9%)
  matrix products  12.4 us (7%)
  local copies, waits for them, and re-layouts  7.21 us (4%)
  other arithmetic  2.22 us (1%)
    all_to_all x2, waiting for transfers between devices, spread(): lax.all_to_all(jnp.broadcast_to(a[None], (peers,) + a.shape), axes, 0, 0,...  25 us
    all_to_all x1, blocking collectives, on_device(): part = lax.all_to_all(part.reshape(16, 16, 128), 'z', 0, 0, tiled=True)  24.6 us
    all_to_all x1, blocking collectives, on_device(): part = lax.all_to_all(part.reshape(16, 16, D_OUT), YX, 0, 0, tiled=True)  22.9 us
    all_to_all x1, blocking collectives, spread(): lax.all_to_all(jnp.broadcast_to(a[None], (peers,) + a.shape), axes, 0, 0,...  21.7 us
    all_to_all x1, blocking collectives, on_device(): sums = lax.all_to_all(own, ('yl', 'c', 'yh', 'x'), 0, 0, tiled=True)  18.8 us
    ppermute x4, starting transfers between devices, other(): return lax.ppermute(a, 'c', swap)  12.5 us
    all_to_all x2, starting transfers between devices, spread(): lax.all_to_all(jnp.broadcast_to(a[None], (peers,) + a.shape), axes, 0, 0,...  11.8 us
    dot_general x1, matrix products, on_device(): lax.dot_general(grad2, weight_half, (((1,), (1,)), ((), ())), preferred_e...  3.79 us
  transfers between devices with their start and end apart: 7, of which 3 were waited for; matrix products, arithmetic and copies ran while one was open for 10% of the time, Pallas kernels for 0%

profile of v1, /device:TPU:1, one launch (start us, length us, event | category | flops | bytes accessed | tf_op | source)
XLA Modules:
  0.0 175.2 jit_solution(3283325783727732565)
XLA Ops:
  7.2 0.0 all-gather.2.cloned.1.call-start
  7.2 1.2 copy-done
  8.4 0.8 constant_dynamic-slice_fusion
  9.3 1.3 fusion.2
  10.7 0.1 copy.12
  10.8 1.0 broadcast_in_dim.32
  11.9 7.5 %all-to-all-start = ((bf16[8,256,256]{2,1,0:T(8,128)(2,1)}), bf16[8,256,256]{2,1,0:T(8,128)(2,1)S(1)}, u32[]{:S(2)}, u32[]{:S(2)}) async-start(bf16[8,256,256]{2,1,0:T(8,128)(2,1)} %broadcast_in_dim.32), calls=%async_computation | async-start | bytes 2097152 | tf_op jit(solution)/shard_map/basis/all_to_all | solution.py:22
  19.4 4.9 %collective-permute-start = (bf16[128,2048]{1,0:T(8,128)(2,1)S(1)}, bf16[128,2048]{1,0:T(8,128)(2,1)S(1)}, u32[]{:S(2)}, u32[]{:S(2)}) collective-permute-start(bf16[128,2048]{1,0:T(8,128)(2,1)S(1)} %copy-done.1), channel_id=1, source_target_pairs={{0,8},{8,0},{1,9},{9,1},{2,10},{10,2},{3,11},{11,3},{4,12},{12,4},... | collective-permute-start | bytes 1572872 | tf_op jit(solution)/shard_map/swap_tokens/ppermute | solution.py:39
  24.3 1.9 %collective-permute-start.2 = (bf16[128,2048]{1,0:T(8,128)(2,1)S(1)}, bf16[128,2048]{1,0:T(8,128)(2,1)}, u32[]{:S(2)}, u32[]{:S(2)}) collective-permute-start(bf16[128,2048]{1,0:T(8,128)(2,1)S(1)} %copy-done.6), channel_id=1, source_target_pairs={{0,8},{8,0},{1,9},{9,1},{2,10},{10,2},{3,11},{11,3},{4,12},{12,4},... | collective-permute-start | bytes 1572872 | tf_op jit(solution)/shard_map/swap_tokens/ppermute | solution.py:39
  26.3 1.0 copy-done.2
  27.3 0.9 collective-permute-done.2
  28.2 8.3 %all-to-all-done = bf16[8,256,256]{2,1,0:T(8,128)(2,1)S(1)} async-done(((bf16[8,256,256]{2,1,0:T(8,128)(2,1)}), bf16[8,256,256]{2,1,0:T(8,128)(2,1)S(1)}, u32[]{:S(2)}, u32[]{:S(2)}) %all-to-all-start) | async-done | bytes 1048608 | tf_op jit(solution)/shard_map/basis/all_to_all | solution.py:22
  36.5 2.9 %convolution_convert_fusion = bf16[256,2048]{1,0:T(8,128)(2,1)S(1)} fusion(bf16[256,2048]{1,0:T(8,128)(2,1)} %copy-done.2, bf16[2048,256]{1,0:T(8,128)(2,1)S(1)} %bitcast.22, bf16[128,2048]{1,0:T(8,128)(2,1)} %collective-permute-done.2, bf16[128,2048]{1,0:T(8,128)(2,1)} %param.6), kind=kOutput, calls=%fused_computation.3 | convolution fusion | flops 539557888 | bytes 4194304 | tf_op jit(solution)/shard_map/projected/dot_general | solution.py:58
  39.5 22.9 %all_to_all.34 = bf16[16,16,2048]{2,1,0:T(8,128)(2,1)S(1)} all-to-all(bf16[16,16,2048]{2,1,0:T(8,128)(2,1)S(1)} %bitcast.23), channel_id=1, replica_groups=mesh['yl'=2,'z'=16,'c'=2,'yh'=2,'x'=4] {'yl','yh','x'}, dimensions={0} | all-to-all | bytes 2097152 | tf_op jit(solution)/shard_map/sum_yx/all_to_all | solution.py:62
  62.4 0.1 convert_reduce_fusion
  62.6 24.6 %all_to_all.35 = f32[16,16,128]{2,1,0:T(8,128)S(1)} all-to-all(f32[16,16,128]{2,1,0:T(8,128)S(1)} %bitcast.25), channel_id=1, replica_groups=mesh['yl'=2,'z'=16,'c'=2,'yh'=2,'x'=4] {'z'}, dimensions={0} | all-to-all | bytes 262144 | tf_op jit(solution)/shard_map/sum_z/all_to_all | solution.py:65
  87.2 21.7 %all_to_all.36 = f32[16,48,128]{2,1,0:T(8,128)S(1)} all-to-all(f32[16,48,128]{2,1,0:T(8,128)S(1)} %broadcast_in_dim.33), channel_id=1, replica_groups=mesh['yl'=2,'z'=16,'c'=2,'yh'=2,'x'=4] {'z'}, dimensions={0} | all-to-all | bytes 786432 | tf_op jit(solution)/shard_map/rows_z/all_to_all | solution.py:22
  108.9 0.6 multiply_reduce_fusion
  109.5 0.7 broadcast_in_dim.34
  110.2 18.8 %all_to_all.37 = f32[32,1,128]{2,1,0:T(1,128)S(1)} all-to-all(f32[32,1,128]{2,1,0:T(1,128)S(1)} %broadcast_in_dim.34), channel_id=1, replica_groups=mesh['yl'=2,'z'=16,'c'=2,'yh'=2,'x'=4] {'yl','c','yh','x'}, dimensions={0} | all-to-all | bytes 32768 | tf_op jit(solution)/shard_map/total/all_to_all | solution.py:74
  129.0 0.6 slice_reduce_fusion
  130.3 0.1 fusion.50
  130.5 1.1 broadcast_in_dim.36
  131.6 4.3 %all-to-all-start.5 = ((bf16[16,16,2048]{2,1,0:T(8,128)(2,1)}), bf16[16,16,2048]{2,1,0:T(8,128)(2,1)}, u32[]{:S(2)}, u32[]{:S(2)}) async-start(bf16[16,16,2048]{2,1,0:T(8,128)(2,1)} %broadcast_in_dim.36), calls=%async_computation.5 | async-start | bytes 2097152 | tf_op jit(solution)/shard_map/rows_yx/all_to_all | solution.py:22
  136.0 16.6 %all-to-all-done.5 = bf16[16,16,2048]{2,1,0:T(8,128)(2,1)} async-done(((bf16[16,16,2048]{2,1,0:T(8,128)(2,1)}), bf16[16,16,2048]{2,1,0:T(8,128)(2,1)}, u32[]{:S(2)}, u32[]{:S(2)}) %all-to-all-start.5) | async-done | bytes 1048608 | tf_op jit(solution)/shard_map/rows_yx/all_to_all | solution.py:22
  152.6 3.8 %collective-permute-start.3 = (bf16[256,2048]{1,0:T(8,128)(2,1)}, bf16[256,2048]{1,0:T(8,128)(2,1)}, u32[]{:S(2)}, u32[]{:S(2)}) collective-permute-start(bf16[256,2048]{1,0:T(8,128)(2,1)} %bitcast.7), channel_id=1, source_target_pairs={{0,8},{8,0},{1,9},{9,1},{2,10},{10,2},{3,11},{11,3},{4,12},{12,4},... | collective-permute-start | bytes 3145736 | tf_op jit(solution)/shard_map/update/ppermute | solution.py:39
  156.4 0.6 fusion.51
  157.0 1.7 fusion.71
  158.7 3.8 %convolution_convert_fusion.1 = bf16[256,1024]{1,0:T(8,128)(2,1)S(1)} fusion(bf16[256,2048]{1,0:T(8,128)(2,1)} %copy-done.2, bf16[1024,2048]{1,0:T(8,128)(2,1)} %all-gather.2.cloned.1.call-done), kind=kOutput, calls=%fused_computation.20 | convolution fusion | flops 1074003968 | bytes 5767168 | tf_op jit(solution)/shard_map/grad_in/dot_general | solution.py:91
  162.6 1.9 %collective-permute-start.1 = (bf16[128,1024]{1,0:T(8,128)(2,1)S(1)}, bf16[128,1024]{1,0:T(8,128)(2,1)S(1)}, u32[]{:S(2)}, u32[]{:S(2)}) collective-permute-start(bf16[128,1024]{1,0:T(8,128)(2,1)S(1)} %slice.98), channel_id=1, source_target_pairs={{0,8},{8,0},{1,9},{9,1},{2,10},{10,2},{3,11},{11,3},{4,12},{12,4},... | collective-permute-start | bytes 786440 | tf_op jit(solution)/shard_map/grad_in/ppermute | solution.py:39
  164.5 2.7 %fusion.1 = bf16[256,2048]{1,0:T(8,128)(2,1)} fusion(f32[256,2048]{1,0:T(8,128)S(1)} %fusion.71, bf16[256,2048]{1,0:T(8,128)(2,1)} %collective-permute-done.3, bf16[256,512]{0,1:T(8,128)(2,1)S(1)} %fusion.2), kind=kOutput, calls=%fused_computation.2 | convolution fusion | flops 270008320 | bytes 4325376 | tf_op jit(solution)/shard_map/update/dot_general | solution.py:88
  167.6 0.8 copy-done.5
  (50 shorter events, 0.7 us)
Async XLA Ops:
  7.2 1.2 copy-start
  7.2 151.5 %all-gather.2.cloned.1.call-start = ((), (), s32[]{:S(2)}) async-start(), calls=%async_computation.6 | async-start | bytes 4718592 | tf_op jit(solution)/shard_map/weight/all_gather | solution.py:55
  10.7 8.7 %copy-start.1 = (bf16[128,2048]{1,0:T(8,128)(2,1)S(1)}, bf16[128,2048]{1,0:T(8,128)(2,1)}, u32[]{:S(2)}) copy-start(bf16[128,2048]{1,0:T(8,128)(2,1)} %param.7) | copy-start | bytes 1572868
  10.7 13.6 %copy-start.6 = (bf16[128,2048]{1,0:T(8,128)(2,1)S(1)}, bf16[128,2048]{1,0:T(8,128)(2,1)}, u32[]{:S(2)}) copy-start(bf16[128,2048]{1,0:T(8,128)(2,1)} %param.6) | copy-start | bytes 1572868
  11.9 24.7 %all-to-all-start = ((bf16[8,256,256]{2,1,0:T(8,128)(2,1)}), bf16[8,256,256]{2,1,0:T(8,128)(2,1)S(1)}, u32[]{:S(2)}, u32[]{:S(2)}) async-start(bf16[8,256,256]{2,1,0:T(8,128)(2,1)} %broadcast_in_dim.32), calls=%async_computation | async-start | bytes 2097152 | tf_op jit(solution)/shard_map/basis/all_to_all | solution.py:22
  19.4 6.9 %collective-permute-start = (bf16[128,2048]{1,0:T(8,128)(2,1)S(1)}, bf16[128,2048]{1,0:T(8,128)(2,1)S(1)}, u32[]{:S(2)}, u32[]{:S(2)}) collective-permute-start(bf16[128,2048]{1,0:T(8,128)(2,1)S(1)} %copy-done.1), channel_id=1, source_target_pairs={{0,8},{8,0},{1,9},{9,1},{2,10},{10,2},{3,11},{11,3},{4,12},{12,4},... | collective-permute-start | bytes 1572872 | tf_op jit(solution)/shard_map/swap_tokens/ppermute | solution.py:39
  24.3 3.9 %collective-permute-start.2 = (bf16[128,2048]{1,0:T(8,128)(2,1)S(1)}, bf16[128,2048]{1,0:T(8,128)(2,1)}, u32[]{:S(2)}, u32[]{:S(2)}) collective-permute-start(bf16[128,2048]{1,0:T(8,128)(2,1)S(1)} %copy-done.6), channel_id=1, source_target_pairs={{0,8},{8,0},{1,9},{9,1},{2,10},{10,2},{3,11},{11,3},{4,12},{12,4},... | collective-permute-start | bytes 1572872 | tf_op jit(solution)/shard_map/swap_tokens/ppermute | solution.py:39
  26.3 1.0 copy-start.2
  39.5 47.7 %copy-start.3 = (f32[1,2048]{1,0:T(1,128)S(1)}, f32[1,2048]{1,0:T(1,128)}, u32[]{:S(2)}) copy-start(f32[1,2048]{1,0:T(1,128)} %param.11) | copy-start | bytes 24580
  39.5 47.7 %copy-start.4 = (f32[1,2048]{1,0:T(1,128)S(1)}, f32[1,2048]{1,0:T(1,128)}, u32[]{:S(2)}) copy-start(f32[1,2048]{1,0:T(1,128)} %param.10) | copy-start | bytes 24580
  131.6 21.0 %all-to-all-start.5 = ((bf16[16,16,2048]{2,1,0:T(8,128)(2,1)}), bf16[16,16,2048]{2,1,0:T(8,128)(2,1)}, u32[]{:S(2)}, u32[]{:S(2)}) async-start(bf16[16,16,2048]{2,1,0:T(8,128)(2,1)} %broadcast_in_dim.36), calls=%async_computation.5 | async-start | bytes 2097152 | tf_op jit(solution)/shard_map/rows_yx/all_to_all | solution.py:22
  152.6 11.9 %collective-permute-start.3 = (bf16[256,2048]{1,0:T(8,128)(2,1)}, bf16[256,2048]{1,0:T(8,128)(2,1)}, u32[]{:S(2)}, u32[]{:S(2)}) collective-permute-start(bf16[256,2048]{1,0:T(8,128)(2,1)} %bitcast.7), channel_id=1, source_target_pairs={{0,8},{8,0},{1,9},{9,1},{2,10},{10,2},{3,11},{11,3},{4,12},{12,4},... | collective-permute-start | bytes 3145736 | tf_op jit(solution)/shard_map/update/ppermute | solution.py:39
  162.6 4.6 %collective-permute-start.1 = (bf16[128,1024]{1,0:T(8,128)(2,1)S(1)}, bf16[128,1024]{1,0:T(8,128)(2,1)S(1)}, u32[]{:S(2)}, u32[]{:S(2)}) collective-permute-start(bf16[128,1024]{1,0:T(8,128)(2,1)S(1)} %slice.98), channel_id=1, source_target_pairs={{0,8},{8,0},{1,9},{9,1},{2,10},{10,2},{3,11},{11,3},{4,12},{12,4},... | collective-permute-start | bytes 786440 | tf_op jit(solution)/shard_map/grad_in/ppermute | solution.py:39
  167.6 0.8 copy-start.5
Sparse Core Ops, SparseCore 0:
  11.8 95.4 all-gather.1

commit v2 on v1

v2 whole, which is shorter than its diff:
```python
import math

import jax
import jax.numpy as jnp
from jax import lax
from jax.experimental import pallas as pl
from jax.experimental.pallas import tpu as pltpu
from jax.sharding import Mesh
from jax.sharding import PartitionSpec as P

D_OUT = 2048
RANK = 512
AXES = ("yl", "z", "c", "yh", "x")
YX = ("yl", "yh", "x")
FSDP = ("yh", "x")
bf16 = jnp.bfloat16
f32 = jnp.float32

first_bias = 1.0 - 0.9**10
second_bias = 1.0 - 0.999**10

ANY = pl.BlockSpec(memory_space=pl.ANY)
VMEM = pl.BlockSpec(memory_space=pltpu.VMEM)
SHORT = pl.CostEstimate(flops=1000, bytes_accessed=1000, transcendentals=0)
LONG = pl.CostEstimate(flops=20_000_000_000, bytes_accessed=1 << 20, transcendentals=0)


def shape(*dims, dtype=bf16):
    return jax.ShapeDtypeStruct(dims, dtype)


def call(body, outs, *args, first=None, cost=LONG):
    specs = [VMEM] * len(args)
    if first is not None:
        args, specs = (first,) + args, [ANY] + specs
    return pl.pallas_call(
        body,
        out_shape=outs,
        in_specs=specs,
        out_specs=(VMEM,) * len(outs) if isinstance(outs, tuple) else VMEM,
        compiler_params=pltpu.CompilerParams(vmem_limit_bytes=32 << 20),
        cost_estimate=cost,
    )(*args)


def half_kernel(_, w_ref, o_ref):
    start = pl.multiple_of(lax.axis_index("c") * 128, 128)
    o_ref[...] = w_ref[pl.ds(start, 128)]


def stack_kernel(_, a_ref, b_ref, o_ref):
    o_ref[:128] = a_ref[...]
    o_ref[128:] = b_ref[...]


def cut_kernel(_, a_ref, b_ref, lower_ref, upper_ref):
    lower_ref[...] = a_ref[:128]
    upper_ref[...] = b_ref[128:]


def backward_kernel(_, grad_ref, other_ref, pair, left, right, lower, upper, here, there):
    y, x = lax.axis_index("yh"), lax.axis_index("x")
    blocks = [(pair, 0, 0, 0), (pair, 1, 1, 0), (left, 0, 0, 3), (left, 1, 1, 3)]
    blocks += [(right, 0, 0, 1), (right, 1, 1, 1), (lower, 0, 0, 2), (upper, 0, 1, 2)]
    for ref, part, dy, dx in blocks:
        block = ((y + dy) % 2) * 4 + (x + dx) % 4
        at = pl.ds(pl.multiple_of(block * 128, 128), 128)
        w = ref[part * 128 : part * 128 + 128]
        for g_ref, o_ref in ((grad_ref, here), (other_ref, there)):
            o_ref[:, at] = lax.dot_general(
                g_ref[...], w, (((1,), (1,)), ((), ())), preferred_element_type=f32
            ).astype(bf16)


def weave_kernel(here_ref, there_ref, out_ref):
    core = lax.axis_index("c")
    for k in range(8):
        at = pl.ds(k * 128, 128)
        mine = pl.ds(pl.multiple_of(k * 256 + core * 128, 128), 128)
        theirs = pl.ds(pl.multiple_of(k * 256 + 128 - core * 128, 128), 128)
        out_ref[:, mine] = here_ref[:, at]
        out_ref[:, theirs] = there_ref[:, at]


def sum_yx_kernel(in_ref, out_ref):
    for j in range(16):
        at = pl.ds(j * 128, 128)
        acc = in_ref[0, :, at].astype(f32)
        for k in range(1, 16):
            acc += in_ref[k, :, at].astype(f32)
        out_ref[:, j, :] = acc


def sum_z_kernel(in_ref, m_ref, v_ref, p_ref, out_ref):
    p = jnp.sum(in_ref[...], 0)
    m, v = m_ref[...], v_ref[...]
    p_ref[...] = p
    for k in range(16):
        out_ref[k, :16] = p
        out_ref[k, 16:32] = m
        out_ref[k, 32:] = v


def squares_kernel(rows_ref, out_ref):
    p = rows_ref[:, :16]
    out_ref[...] = jnp.full((32, 128), jnp.sum(p * p), f32)


def adam(p, m, v, factor):
    clipped = factor * p
    first_new = 0.9 * m + 0.1 * clipped
    second_new = 0.999 * v + 0.001 * clipped * clipped
    return first_new, second_new


def adam_kernel(sums_ref, rows_ref, p_ref, m_ref, v_ref, out_ref, first_ref, second_ref):
    total = jnp.sum(sums_ref[...], 0, keepdims=True)
    limit = math.sqrt(RANK * D_OUT)
    factor = jnp.minimum(1.0, limit / (jnp.sqrt(total) + 1e-06))
    first_ref[...], second_ref[...] = adam(p_ref[...], m_ref[...], v_ref[...], factor)
    for j in range(16):
        p, m, v = (rows_ref[:, 16 * t + j, :] for t in range(3))
        f, s = adam(p, m, v, factor)
        d = (f / first_bias / (jnp.sqrt(s / second_bias) + 1e-08)).astype(bf16)
        for k in range(16):
            out_ref[k, :, pl.ds(j * 128, 128)] = d


def spread(a, axes, peers):
    return exchange(jnp.broadcast_to(a[None], (peers,) + a.shape), axes)


def exchange(a, axes):
    return lax.all_to_all(a, axes, 0, 0, tiled=True)


def shift(a, k):
    return lax.ppermute(a, "x", [(i, (i + k) % 4) for i in range(4)])


def on_device(acts, grad_out, weight, basis, first_moment, second_moment):
    core = lax.axis_index("c")
    swap = [(0, 1), (1, 0)]

    def other(a):
        return lax.ppermute(a, "c", swap)

    with jax.named_scope("pick"):
        col = lax.broadcasted_iota(jnp.int32, (RANK, RANK), 1)
        row = lax.broadcasted_iota(jnp.int32, (RANK, RANK), 0)
        own = jnp.where(col < 256, core, 1 - core)
        z, x, yh, yl = col % 16, (col // 16) % 4, (col // 64) % 2, (col // 128) % 2
        pick = (row == (((yl * 16 + z) * 2 + own) * 2 + yh) * 4 + x).astype(bf16)
        basis_p = jnp.dot(basis, pick, preferred_element_type=f32).astype(bf16)
    with jax.named_scope("swap_tokens"):
        grad_other = other(grad_out)
        acts2 = jnp.concatenate([acts, other(acts)], 0)
        grad2 = jnp.concatenate([grad_out, grad_other], 0)
    with jax.named_scope("basis"):
        basis_all = spread(basis_p[:, :256], FSDP, 8).reshape(2048, 256)
    with jax.named_scope("projected"):
        coords = jnp.dot(acts2, basis_all, preferred_element_type=f32).astype(bf16)
        part = lax.dot_general(
            coords, grad2, (((0,), (0,)), ((), ())), preferred_element_type=f32
        ).astype(bf16)
    with jax.named_scope("weight_y"):
        half = call(half_kernel, shape(128, 2048), weight, first=part)
        cross = lax.ppermute(half, "yh", swap)
    with jax.named_scope("sum_yx"):
        part = exchange(part.reshape(16, 16, D_OUT), YX)
        part, half = lax.optimization_barrier((part, half))
        part = call(sum_yx_kernel, shape(16, 16, 128, dtype=f32), part)
    with jax.named_scope("weight_x"):
        pair = call(stack_kernel, shape(256, 2048), half, cross, first=part)
        left, right = shift(pair, 1), shift(pair, 3)
    with jax.named_scope("sum_z"):
        part = exchange(part, "z")
        part, pair = lax.optimization_barrier((part, pair))
    m = first_moment.reshape(16, 128)
    v = second_moment.reshape(16, 128)
    with jax.named_scope("rows_z"):
        p, rows = call(
            sum_z_kernel,
            (shape(16, 128, dtype=f32), shape(16, 48, 128, dtype=f32)),
            part, m, v,
        )
    with jax.named_scope("weight_far"):
        low, high = call(cut_kernel, (shape(128, 2048),) * 2, left, right, first=p)
        lower, upper = shift(low, 1), shift(high, 3)
    with jax.named_scope("rows_z"):
        rows = exchange(rows, "z")
        rows, low, high = lax.optimization_barrier((rows, low, high))
    with jax.named_scope("total"):
        sums = exchange(call(squares_kernel, shape(32, 128, dtype=f32), rows), ("yl", "c", "yh", "x"))
    with jax.named_scope("adam"):
        direction, first_new, second_new = call(
            adam_kernel,
            (shape(16, 16, D_OUT), shape(16, 128, dtype=f32), shape(16, 128, dtype=f32)),
            sums, rows, p, m, v,
        )
    with jax.named_scope("grad_in"):
        here, there = call(
            backward_kernel,
            (shape(128, 1024),) * 2,
            grad_out, grad_other, pair, left, right, lower, upper,
            first=direction,
        )
        grad_in = call(weave_kernel, shape(128, D_OUT), here, other(there), cost=SHORT)
    with jax.named_scope("rows_yx"):
        mine = exchange(direction, YX).reshape(256, D_OUT)
        mine, grad_in = lax.optimization_barrier((mine, grad_in))
    with jax.named_scope("update"):
        theirs = other(mine)
        update = jnp.dot(basis_p[:, :256], mine, preferred_element_type=f32)
        update = update + jnp.dot(basis_p[:, 256:], theirs, preferred_element_type=f32)
        weight_update = (0.25 * update).astype(bf16)
    return (
        grad_in,
        first_new.reshape(1, D_OUT),
        second_new.reshape(1, D_OUT),
        weight_update,
    )


def solution(mesh):
    fine = Mesh(mesh.devices.reshape(2, 16, 2, 2, 4), AXES)
    rows = P(AXES, None)
    shared = P(FSDP, None)
    return jax.shard_map(
        on_device,
        mesh=fine,
        in_specs=(rows, rows, shared, shared, rows, rows),
        out_specs=(rows, rows, rows, shared),
        check_vma=False,
    )
```

time: 176 us -> 157 us (0.89)
  blocking collectives: 87.9 us -> 0 us
  starting transfers between devices: 24.3 us -> 83.9 us
  waiting for transfers between devices: 25.9 us -> 49.2 us
  between operations: 15.2 us -> 0.93 us
  Pallas kernels: 0 us -> 10.1 us
  matrix products: 12.4 us -> 5.87 us
  other arithmetic: 2.22 us -> 0.04 us
  local copies, waits for them, and re-layouts: 7.21 us -> 5.38 us
    all_to_all x4 -> x0, blocking collectives: 87.9 us -> none  [the longest x1 24.6 us: on_device(): part = lax.all_to_all(part.reshape(16, 16, 128), 'z', 0, 0, tiled=True)]
    all_to_all x2 -> x6, starting transfers between devices: 11.8 us -> 51.3 us  [exchange(): return lax.all_to_all(a, axes, 0, 0, tiled=True)]
    ppermute x0 -> x5, starting transfers between devices: none -> 16.5 us  [the longest x4 11.8 us: shift(): return lax.ppermute(a, 'x', [(i, (i + k) % 4) for i in range(4)])]
    ppermute x0 -> x5, waiting for transfers between devices: none -> 13.8 us  [the longest x4 13.8 us: shift(): return lax.ppermute(a, 'x', [(i, (i + k) % 4) for i in range(4)])]
    pallas_call x0 -> x9, Pallas kernels: none -> 10.1 us  [call(): pl.pallas_call(body, out_shape=outs, in_specs=specs, out_specs=(VMEM,) *...]
    all_to_all x2 -> x6, waiting for transfers between devices: 25 us -> 29.9 us  [exchange(): return lax.all_to_all(a, axes, 0, 0, tiled=True)]
    ppermute x4, waiting for transfers between devices: 0.93 us -> 5.49 us  [other(): return lax.ppermute(a, 'c', swap)]
    dot_general x1 -> x0, matrix products: 3.79 us -> none  [on_device(): lax.dot_general(grad2, weight_half, (((1,), (1,)), ((), ())), preferred_e...]
  transfers between devices with their start and end apart: 7 -> 15, of which waited for: 3 -> 12; matrix products, arithmetic and copies ran while one was open for 10% -> 0% of each run, Pallas kernels for 0% -> 6%
where the time goes in v2:
time: 157 us; the launch traced here: 155 us
  starting transfers between devices  83.9 us (53%)
  waiting for transfers between devices  49.2 us (31%)
  Pallas kernels  10.1 us (6%)
  matrix products  5.87 us (4%)
  local copies, waits for them, and re-layouts  5.38 us (3%)
    all_to_all x6, starting transfers between devices, exchange(): return lax.all_to_all(a, axes, 0, 0, tiled=True)  51.3 us
    all_to_all x6, waiting for transfers between devices, exchange(): return lax.all_to_all(a, axes, 0, 0, tiled=True)  29.9 us
    ppermute x4, starting transfers between devices, other(): return lax.ppermute(a, 'c', swap)  16.2 us
    ppermute x4, waiting for transfers between devices, shift(): return lax.ppermute(a, 'x', [(i, (i + k) % 4) for i in range(4)])  13.8 us
    ppermute x4, starting transfers between devices, shift(): return lax.ppermute(a, 'x', [(i, (i + k) % 4) for i in range(4)])  11.8 us
    pallas_call x9, Pallas kernels, call(): pl.pallas_call(body, out_shape=outs, in_specs=specs, out_specs=(VMEM,) *...  10.1 us
    ppermute x4, waiting for transfers between devices, other(): return lax.ppermute(a, 'c', swap)  5.49 us
    ppermute x1, starting transfers between devices, on_device(): cross = lax.ppermute(half, 'yh', swap)  4.67 us
  transfers between devices with their start and end apart: 15, of which 12 were waited for; matrix products, arithmetic and copies ran while one was open for 0% of the time, Pallas kernels for 6%

profile of v2, /device:TPU:1, one launch (start us, length us, event | category | flops | bytes accessed | tf_op | source)
XLA Modules:
  0.0 155.4 jit_solution(10107512128928230261)
XLA Ops:
  3.8 7.5 %all-to-all-start = ((bf16[8,256,256]{2,1,0:T(8,128)(2,1)}), bf16[8,256,256]{2,1,0:T(8,128)(2,1)S(1)}, u32[]{:S(2)}, u32[]{:S(2)}) async-start(bf16[8,256,256]{2,1,0:T(8,128)(2,1)} %broadcast_in_dim.16), calls=%async_computation | async-start | bytes 2097152 | tf_op jit(solution)/shard_map/basis/all_to_all | solution.py:134
  11.3 4.9 %collective-permute-start = (bf16[128,2048]{1,0:T(8,128)(2,1)S(1)}, bf16[128,2048]{1,0:T(8,128)(2,1)S(1)}, u32[]{:S(2)}, u32[]{:S(2)}) collective-permute-start(bf16[128,2048]{1,0:T(8,128)(2,1)S(1)} %copy-done.11), channel_id=1, source_target_pairs={{0,8},{8,0},{1,9},{9,1},{2,10},{10,2},{3,11},{11,3},{4,12},{12,4},... | collective-permute-start | bytes 1572872 | tf_op jit(solution)/shard_map/swap_tokens/ppermute | solution.py:146
  16.2 1.9 %collective-permute-start.1 = (bf16[128,2048]{1,0:T(8,128)(2,1)S(1)}, bf16[128,2048]{1,0:T(8,128)(2,1)S(1)}, u32[]{:S(2)}, u32[]{:S(2)}) collective-permute-start(bf16[128,2048]{1,0:T(8,128)(2,1)S(1)} %copy-done.2), channel_id=1, source_target_pairs={{0,8},{8,0},{1,9},{9,1},{2,10},{10,2},{3,11},{11,3},{4,12},{12,4},... | collective-permute-start | bytes 1572872 | tf_op jit(solution)/shard_map/swap_tokens/ppermute | solution.py:146
  18.2 1.9 %collective-permute-done.1.other_ref = bf16[128,2048]{1,0:T(8,128)(2,1)S(1)} collective-permute-done((bf16[128,2048]{1,0:T(8,128)(2,1)S(1)}, bf16[128,2048]{1,0:T(8,128)(2,1)S(1)}, u32[]{:S(2)}, u32[]{:S(2)}) %collective-permute-start.1) | collective-permute-done | bytes 524320 | tf_op jit(solution)/shard_map/swap_tokens/ppermute | solution.py:146
  20.0 8.5 %all-to-all-done = bf16[8,256,256]{2,1,0:T(8,128)(2,1)S(1)} async-done(((bf16[8,256,256]{2,1,0:T(8,128)(2,1)}), bf16[8,256,256]{2,1,0:T(8,128)(2,1)S(1)}, u32[]{:S(2)}, u32[]{:S(2)}) %all-to-all-start) | async-done | bytes 1048608 | tf_op jit(solution)/shard_map/basis/all_to_all | solution.py:134
  28.5 2.4 %convolution_convert_fusion._ = bf16[256,2048]{1,0:T(8,128)(2,1)} fusion(bf16[2048,256]{1,0:T(8,128)(2,1)S(1)} %bitcast.22, bf16[128,2048]{1,0:T(8,128)(2,1)S(1)} %collective-permute-done, bf16[128,2048]{1,0:T(8,128)(2,1)S(1)} %copy-done.11, bf16[128,2048]{1,0:T(8,128)(2,1)S(1)} %collective-permute-done.1.other_ref, bf16[128,2048]{1,0:T(8,128)(2,1)S(1)} %copy-done.2), kind=kOutput, calls=%fused_computation.3 | convolution fusion | flops 541655040 | bytes 4194304 | tf_op jit(solution)/shard_map/projected/dot_general | solution.py:163
  30.9 3.8 %all-to-all-start.1 = ((bf16[16,16,2048]{2,1,0:T(8,128)(2,1)}), bf16[16,16,2048]{2,1,0:T(8,128)(2,1)S(1)}, u32[]{:S(2)}, u32[]{:S(2)}) async-start(bf16[16,16,2048]{2,1,0:T(8,128)(2,1)} %bitcast.2), calls=%async_computation.1 | async-start | bytes 2097152 | tf_op jit(solution)/shard_map/sum_yx/all_to_all | solution.py:134
  34.7 4.7 %collective-permute-start.2 = (bf16[128,2048]{1,0:T(8,128)(2,1)S(1)}, bf16[128,2048]{1,0:T(8,128)(2,1)S(1)}, u32[]{:S(2)}, u32[]{:S(2)}) collective-permute-start(bf16[128,2048]{1,0:T(8,128)(2,1)S(1)} %weight_y.1.a_ref), channel_id=1, source_target_pairs={{0,4},{4,0},{1,5},{5,1},{2,6},{6,2},{3,7},{7,3},{8,12},{12,8},{9,1... | collective-permute-start | bytes 1572872 | tf_op jit(solution)/shard_map/weight_y/ppermute | solution.py:168
  39.4 11.8 %all-to-all-done.1.in_ref = bf16[16,16,2048]{2,1,0:T(8,128)(2,1)S(1)} async-done(((bf16[16,16,2048]{2,1,0:T(8,128)(2,1)}), bf16[16,16,2048]{2,1,0:T(8,128)(2,1)S(1)}, u32[]{:S(2)}, u32[]{:S(2)}) %all-to-all-start.1) | async-done | bytes 1048608 | tf_op jit(solution)/shard_map/sum_yx/all_to_all | solution.py:134
  52.1 15.3 %all-to-all-start.2 = ((f32[16,16,128]{2,1,0:T(8,128)}), f32[16,16,128]{2,1,0:T(8,128)S(1)}, u32[]{:S(2)}, u32[]{:S(2)}) async-start(f32[16,16,128]{2,1,0:T(8,128)} %sum_yx.1._), calls=%async_computation.2 | async-start | bytes 262144 | tf_op jit(solution)/shard_map/sum_z/all_to_all | solution.py:134
  67.5 1.9 %collective-permute-start.4 = (bf16[256,2048]{1,0:T(8,128)(2,1)S(1)}, bf16[256,2048]{1,0:T(8,128)(2,1)S(1)}, u32[]{:S(2)}, u32[]{:S(2)}) collective-permute-start(bf16[256,2048]{1,0:T(8,128)(2,1)S(1)} %weight_x.1.pair), channel_id=1, source_target_pairs={{0,3},{1,0},{2,1},{3,2},{4,7},{5,4},{6,5},{7,6},{8,11},{9,8},{10,9... | collective-permute-start | bytes 3145736 | tf_op jit(solution)/shard_map/weight_x/ppermute | solution.py:138
  69.4 3.4 %collective-permute-start.3 = (bf16[256,2048]{1,0:T(8,128)(2,1)S(1)}, bf16[256,2048]{1,0:T(8,128)(2,1)}, u32[]{:S(2)}, u32[]{:S(2)}) collective-permute-start(bf16[256,2048]{1,0:T(8,128)(2,1)S(1)} %weight_x.1.pair), channel_id=1, source_target_pairs={{0,1},{1,2},{2,3},{3,0},{4,5},{5,6},{6,7},{7,4},{8,9},{9,10},{10,1... | collective-permute-start | bytes 3145736 | tf_op jit(solution)/shard_map/weight_x/ppermute | solution.py:138
  72.8 6.7 %all-to-all-done.2.in_ref = f32[16,16,128]{2,1,0:T(8,128)S(1)} async-done(((f32[16,16,128]{2,1,0:T(8,128)}), f32[16,16,128]{2,1,0:T(8,128)S(1)}, u32[]{:S(2)}, u32[]{:S(2)}) %all-to-all-start.2) | async-done | bytes 131104 | tf_op jit(solution)/shard_map/sum_z/all_to_all | solution.py:134
  80.2 4.8 %all-to-all-start.3 = ((f32[16,48,128]{2,1,0:T(8,128)}), f32[16,48,128]{2,1,0:T(8,128)S(1)}, u32[]{:S(2)}, u32[]{:S(2)}) async-start(f32[16,48,128]{2,1,0:T(8,128)} %get-tuple-element.23), calls=%async_computation.3 | async-start | bytes 786432 | tf_op jit(solution)/shard_map/rows_z/all_to_all | solution.py:134
  85.1 6.2 %collective-permute-done.4.b_ref.right = bf16[256,2048]{1,0:T(8,128)(2,1)S(1)} collective-permute-done((bf16[256,2048]{1,0:T(8,128)(2,1)S(1)}, bf16[256,2048]{1,0:T(8,128)(2,1)S(1)}, u32[]{:S(2)}, u32[]{:S(2)}) %collective-permute-start.4) | collective-permute-done | bytes 1048608 | tf_op jit(solution)/shard_map/weight_x/ppermute | solution.py:138
  91.3 2.9 %collective-permute-done.3.a_ref.left = bf16[256,2048]{1,0:T(8,128)(2,1)} collective-permute-done((bf16[256,2048]{1,0:T(8,128)(2,1)S(1)}, bf16[256,2048]{1,0:T(8,128)(2,1)}, u32[]{:S(2)}, u32[]{:S(2)}) %collective-permute-start.3) | collective-permute-done | bytes 1048608 | tf_op jit(solution)/shard_map/weight_x/ppermute | solution.py:138
  94.2 1.3 weight_far.1
  97.1 2.7 %all-to-all-done.3.rows_ref = f32[16,48,128]{2,1,0:T(8,128)S(1)} async-done(((f32[16,48,128]{2,1,0:T(8,128)}), f32[16,48,128]{2,1,0:T(8,128)S(1)}, u32[]{:S(2)}, u32[]{:S(2)}) %all-to-all-start.3) | async-done | bytes 393248 | tf_op jit(solution)/shard_map/rows_z/all_to_all | solution.py:134
  100.5 14.6 %all-to-all-start.4 = ((f32[32,1,128]{2,1,0:T(1,128)}), f32[32,1,128]{2,1,0:T(1,128)S(1)}, u32[]{:S(2)}, u32[]{:S(2)}) async-start(f32[32,1,128]{2,1,0:T(1,128)} %bitcast.6), calls=%async_computation.4 | async-start | bytes 32768 | tf_op jit(solution)/shard_map/total/all_to_all | solution.py:134
  115.1 3.3 %collective-permute-start.5 = (bf16[128,2048]{1,0:T(8,128)(2,1)}, bf16[128,2048]{1,0:T(8,128)(2,1)}, u32[]{:S(2)}, u32[]{:S(2)}) collective-permute-start(bf16[128,2048]{1,0:T(8,128)(2,1)} %copy-done.6), channel_id=1, source_target_pairs={{0,1},{1,2},{2,3},{3,0},{4,5},{5,6},{6,7},{7,4},{8,9},{9,10},{10,1... | collective-permute-start | bytes 1572872 | tf_op jit(solution)/shard_map/weight_far/ppermute | solution.py:138
  118.4 3.2 %collective-permute-start.6 = (bf16[128,2048]{1,0:T(8,128)(2,1)}, bf16[128,2048]{1,0:T(8,128)(2,1)}, u32[]{:S(2)}, u32[]{:S(2)}) collective-permute-start(bf16[128,2048]{1,0:T(8,128)(2,1)} %copy-done.5), channel_id=1, source_target_pairs={{0,3},{1,0},{2,1},{3,2},{4,7},{5,4},{6,5},{7,6},{8,11},{9,8},{10,9... | collective-permute-start | bytes 1572872 | tf_op jit(solution)/shard_map/weight_far/ppermute | solution.py:138
  121.9 1.5 adam.1
  123.4 5.3 %all-to-all-start.5 = ((bf16[16,16,2048]{2,1,0:T(8,128)(2,1)}), bf16[16,16,2048]{2,1,0:T(8,128)(2,1)}, u32[]{:S(2)}, u32[]{:S(2)}) async-start(bf16[16,16,2048]{2,1,0:T(8,128)(2,1)} %get-tuple-element.28._), calls=%async_computation.5 | async-start | bytes 2097152 | tf_op jit(solution)/shard_map/rows_yx/all_to_all | solution.py:134
  128.8 3.0 %collective-permute-done.5.lower = bf16[128,2048]{1,0:T(8,128)(2,1)} collective-permute-done((bf16[128,2048]{1,0:T(8,128)(2,1)}, bf16[128,2048]{1,0:T(8,128)(2,1)}, u32[]{:S(2)}, u32[]{:S(2)}) %collective-permute-start.5) | collective-permute-done | bytes 524320 | tf_op jit(solution)/shard_map/weight_far/ppermute | solution.py:138
  131.8 1.6 %collective-permute-done.6.upper = bf16[128,2048]{1,0:T(8,128)(2,1)} collective-permute-done((bf16[128,2048]{1,0:T(8,128)(2,1)}, bf16[128,2048]{1,0:T(8,128)(2,1)}, u32[]{:S(2)}, u32[]{:S(2)}) %collective-permute-start.6) | collective-permute-done | bytes 524320 | tf_op jit(solution)/shard_map/weight_far/ppermute | solution.py:138
  133.4 1.0 copy-done.4
  134.5 3.8 %grad_in.2 = (bf16[128,1024]{1,0:T(8,128)(2,1)S(1)}, bf16[128,1024]{1,0:T(8,128)(2,1)S(1)}) custom-call(bf16[16,16,2048]{2,1,0:T(8,128)(2,1)} %get-tuple-element.28._, bf16[128,2048]{1,0:T(8,128)(2,1)S(1)} %copy-done.2, bf16[128,2048]{1,0:T(8,128)(2,1)S(1)} %copy-done.4, bf16[256,2048]{1,0:T(8,128)(2,1)S(1)} %weight_x.1.pair, ...), custom_call_target="tpu_custom_call" | custom-call | flops 20000000000 | bytes 1048576 | tf_op jit(solution)/shard_map/grad_in/pallas_call | solution.py:36
  138.3 7.1 %collective-permute-start.7 = (bf16[128,1024]{1,0:T(8,128)(2,1)S(1)}, bf16[128,1024]{1,0:T(8,128)(2,1)S(1)}, u32[]{:S(2)}, u32[]{:S(2)}) collective-permute-start(bf16[128,1024]{1,0:T(8,128)(2,1)S(1)} %get-tuple-element.31), channel_id=1, source_target_pairs={{0,8},{8,0},{1,9},{9,1},{2,10},{10,2},{3,11},{11,3},{4,12},{12,4},... | collective-permute-start | bytes 786440 | tf_op jit(solution)/shard_map/grad_in/ppermute | solution.py:146
  145.5 1.1 collective-permute-done.7.there_ref
  147.5 2.3 %collective-permute-start.8 = (bf16[256,2048]{1,0:T(8,128)(2,1)}, bf16[256,2048]{1,0:T(8,128)(2,1)S(1)}, u32[]{:S(2)}, u32[]{:S(2)}) collective-permute-start(bf16[256,2048]{1,0:T(8,128)(2,1)} %bitcast.8), channel_id=1, source_target_pairs={{0,8},{8,0},{1,9},{9,1},{2,10},{10,2},{3,11},{11,3},{4,12},{12,4},... | collective-permute-start | bytes 3145736 | tf_op jit(solution)/shard_map/update/ppermute | solution.py:146
  149.8 2.5 %collective-permute-done.8 = bf16[256,2048]{1,0:T(8,128)(2,1)S(1)} collective-permute-done((bf16[256,2048]{1,0:T(8,128)(2,1)}, bf16[256,2048]{1,0:T(8,128)(2,1)S(1)}, u32[]{:S(2)}, u32[]{:S(2)}) %collective-permute-start.8) | collective-permute-done | bytes 1048608 | tf_op jit(solution)/shard_map/update/ppermute | solution.py:146
  152.7 2.7 %fusion.1 = bf16[256,2048]{1,0:T(8,128)(2,1)} fusion(f32[256,2048]{1,0:T(8,128)S(1)} %fusion.45, bf16[256,2048]{1,0:T(8,128)(2,1)} %bitcast.8, bf16[256,512]{0,1:T(8,128)(2,1)S(1)} %copy-done.10), kind=kOutput, calls=%fused_computation.2 | convolution fusion | flops 270008320 | bytes 4325376 | tf_op jit(solution)/shard_map/update/dot_general | solution.py:214
  (45 shorter events, 9.0 us)
Async XLA Ops:
  0.6 1.0 copy-start
  2.0 0.7 copy-start.9
  2.7 8.6 %copy-start.11 = (bf16[128,2048]{1,0:T(8,128)(2,1)S(1)}, bf16[128,2048]{1,0:T(8,128)(2,1)}, u32[]{:S(2)}) copy-start(bf16[128,2048]{1,0:T(8,128)(2,1)} %param.6) | copy-start | bytes 1572868
  2.7 13.5 %copy-start.2 = (bf16[128,2048]{1,0:T(8,128)(2,1)S(1)}, bf16[128,2048]{1,0:T(8,128)(2,1)}, u32[]{:S(2)}) copy-start(bf16[128,2048]{1,0:T(8,128)(2,1)} %grad_ref.1) | copy-start | bytes 1572868
  3.8 24.7 %all-to-all-start = ((bf16[8,256,256]{2,1,0:T(8,128)(2,1)}), bf16[8,256,256]{2,1,0:T(8,128)(2,1)S(1)}, u32[]{:S(2)}, u32[]{:S(2)}) async-start(bf16[8,256,256]{2,1,0:T(8,128)(2,1)} %broadcast_in_dim.16), calls=%async_computation | async-start | bytes 2097152 | tf_op jit(solution)/shard_map/basis/all_to_all | solution.py:134
  11.3 6.8 %collective-permute-start = (bf16[128,2048]{1,0:T(8,128)(2,1)S(1)}, bf16[128,2048]{1,0:T(8,128)(2,1)S(1)}, u32[]{:S(2)}, u32[]{:S(2)}) collective-permute-start(bf16[128,2048]{1,0:T(8,128)(2,1)S(1)} %copy-done.11), channel_id=1, source_target_pairs={{0,8},{8,0},{1,9},{9,1},{2,10},{10,2},{3,11},{11,3},{4,12},{12,4},... | collective-permute-start | bytes 1572872 | tf_op jit(solution)/shard_map/swap_tokens/ppermute | solution.py:146
  16.2 3.8 %collective-permute-start.1 = (bf16[128,2048]{1,0:T(8,128)(2,1)S(1)}, bf16[128,2048]{1,0:T(8,128)(2,1)S(1)}, u32[]{:S(2)}, u32[]{:S(2)}) collective-permute-start(bf16[128,2048]{1,0:T(8,128)(2,1)S(1)} %copy-done.2), channel_id=1, source_target_pairs={{0,8},{8,0},{1,9},{9,1},{2,10},{10,2},{3,11},{11,3},{4,12},{12,4},... | collective-permute-start | bytes 1572872 | tf_op jit(solution)/shard_map/swap_tokens/ppermute | solution.py:146
  20.0 10.8 %copy-start.3 = (bf16[128,2048]{1,0:T(8,128)(2,1)}, bf16[128,2048]{1,0:T(8,128)(2,1)S(1)}, u32[]{:S(2)}) copy-start(bf16[128,2048]{1,0:T(8,128)(2,1)S(1)} %collective-permute-done.1.other_ref) | copy-start | bytes 1572868
  30.9 3.8 %copy-start.1 = (bf16[256,2048]{1,0:T(8,128)(2,1)S(1)}, bf16[256,2048]{1,0:T(8,128)(2,1)}, u32[]{:S(2)}) copy-start(bf16[256,2048]{1,0:T(8,128)(2,1)} %w_ref.1) | copy-start | bytes 3145732
  30.9 20.3 %all-to-all-start.1 = ((bf16[16,16,2048]{2,1,0:T(8,128)(2,1)}), bf16[16,16,2048]{2,1,0:T(8,128)(2,1)S(1)}, u32[]{:S(2)}, u32[]{:S(2)}) async-start(bf16[16,16,2048]{2,1,0:T(8,128)(2,1)} %bitcast.2), calls=%async_computation.1 | async-start | bytes 2097152 | tf_op jit(solution)/shard_map/sum_yx/all_to_all | solution.py:134
  34.7 32.7 %collective-permute-start.2 = (bf16[128,2048]{1,0:T(8,128)(2,1)S(1)}, bf16[128,2048]{1,0:T(8,128)(2,1)S(1)}, u32[]{:S(2)}, u32[]{:S(2)}) collective-permute-start(bf16[128,2048]{1,0:T(8,128)(2,1)S(1)} %weight_y.1.a_ref), channel_id=1, source_target_pairs={{0,4},{4,0},{1,5},{5,1},{2,6},{6,2},{3,7},{7,3},{8,12},{12,8},{9,1... | collective-permute-start | bytes 1572872 | tf_op jit(solution)/shard_map/weight_y/ppermute | solution.py:168
  52.1 27.4 %all-to-all-start.2 = ((f32[16,16,128]{2,1,0:T(8,128)}), f32[16,16,128]{2,1,0:T(8,128)S(1)}, u32[]{:S(2)}, u32[]{:S(2)}) async-start(f32[16,16,128]{2,1,0:T(8,128)} %sum_yx.1._), calls=%async_computation.2 | async-start | bytes 262144 | tf_op jit(solution)/shard_map/sum_z/all_to_all | solution.py:134
  67.4 12.1 %copy-start.7 = (f32[1,2048]{1,0:T(1,128)S(1)}, f32[1,2048]{1,0:T(1,128)}, u32[]{:S(2)}) copy-start(f32[1,2048]{1,0:T(1,128)} %param.10) | copy-start | bytes 24580
  67.4 12.1 %copy-start.8 = (f32[1,2048]{1,0:T(1,128)S(1)}, f32[1,2048]{1,0:T(1,128)}, u32[]{:S(2)}) copy-start(f32[1,2048]{1,0:T(1,128)} %param.11) | copy-start | bytes 24580
  67.5 23.8 %collective-permute-start.4 = (bf16[256,2048]{1,0:T(8,128)(2,1)S(1)}, bf16[256,2048]{1,0:T(8,128)(2,1)S(1)}, u32[]{:S(2)}, u32[]{:S(2)}) collective-permute-start(bf16[256,2048]{1,0:T(8,128)(2,1)S(1)} %weight_x.1.pair), channel_id=1, source_target_pairs={{0,3},{1,0},{2,1},{3,2},{4,7},{5,4},{6,5},{7,6},{8,11},{9,8},{10,9... | collective-permute-start | bytes 3145736 | tf_op jit(solution)/shard_map/weight_x/ppermute | solution.py:138
  69.4 24.8 %collective-permute-start.3 = (bf16[256,2048]{1,0:T(8,128)(2,1)S(1)}, bf16[256,2048]{1,0:T(8,128)(2,1)}, u32[]{:S(2)}, u32[]{:S(2)}) collective-permute-start(bf16[256,2048]{1,0:T(8,128)(2,1)S(1)} %weight_x.1.pair), channel_id=1, source_target_pairs={{0,1},{1,2},{2,3},{3,0},{4,5},{5,6},{6,7},{7,4},{8,9},{9,10},{10,1... | collective-permute-start | bytes 3145736 | tf_op jit(solution)/shard_map/weight_x/ppermute | solution.py:138
  80.2 19.5 %all-to-all-start.3 = ((f32[16,48,128]{2,1,0:T(8,128)}), f32[16,48,128]{2,1,0:T(8,128)S(1)}, u32[]{:S(2)}, u32[]{:S(2)}) async-start(f32[16,48,128]{2,1,0:T(8,128)} %get-tuple-element.23), calls=%async_computation.3 | async-start | bytes 786432 | tf_op jit(solution)/shard_map/rows_z/all_to_all | solution.py:134
  95.5 0.8 copy-start.5
  96.3 0.8 copy-start.6
  100.5 21.4 %all-to-all-start.4 = ((f32[32,1,128]{2,1,0:T(1,128)}), f32[32,1,128]{2,1,0:T(1,128)S(1)}, u32[]{:S(2)}, u32[]{:S(2)}) async-start(f32[32,1,128]{2,1,0:T(1,128)} %bitcast.6), calls=%async_computation.4 | async-start | bytes 32768 | tf_op jit(solution)/shard_map/total/all_to_all | solution.py:134
  115.1 16.7 %collective-permute-start.5 = (bf16[128,2048]{1,0:T(8,128)(2,1)}, bf16[128,2048]{1,0:T(8,128)(2,1)}, u32[]{:S(2)}, u32[]{:S(2)}) collective-permute-start(bf16[128,2048]{1,0:T(8,128)(2,1)} %copy-done.6), channel_id=1, source_target_pairs={{0,1},{1,2},{2,3},{3,0},{4,5},{5,6},{6,7},{7,4},{8,9},{9,10},{10,1... | collective-permute-start | bytes 1572872 | tf_op jit(solution)/shard_map/weight_far/ppermute | solution.py:138
  118.4 15.0 %collective-permute-start.6 = (bf16[128,2048]{1,0:T(8,128)(2,1)}, bf16[128,2048]{1,0:T(8,128)(2,1)}, u32[]{:S(2)}, u32[]{:S(2)}) collective-permute-start(bf16[128,2048]{1,0:T(8,128)(2,1)} %copy-done.5), channel_id=1, source_target_pairs={{0,3},{1,0},{2,1},{3,2},{4,7},{5,4},{6,5},{7,6},{8,11},{9,8},{10,9... | collective-permute-start | bytes 1572872 | tf_op jit(solution)/shard_map/weight_far/ppermute | solution.py:138
  123.4 28.9 %copy-start.10 = (bf16[256,512]{0,1:T(8,128)(2,1)S(1)}, bf16[256,512]{0,1:T(8,128)(2,1)}, u32[]{:S(2)}) copy-start(bf16[256,512]{0,1:T(8,128)(2,1)} %copy-done.9) | copy-start | bytes 786436
  123.4 24.1 %all-to-all-start.5 = ((bf16[16,16,2048]{2,1,0:T(8,128)(2,1)}), bf16[16,16,2048]{2,1,0:T(8,128)(2,1)}, u32[]{:S(2)}, u32[]{:S(2)}) async-start(bf16[16,16,2048]{2,1,0:T(8,128)(2,1)} %get-tuple-element.28._), calls=%async_computation.5 | async-start | bytes 2097152 | tf_op jit(solution)/shard_map/rows_yx/all_to_all | solution.py:134
  133.4 1.0 copy-start.4
  138.3 8.3 %collective-permute-start.7 = (bf16[128,1024]{1,0:T(8,128)(2,1)S(1)}, bf16[128,1024]{1,0:T(8,128)(2,1)S(1)}, u32[]{:S(2)}, u32[]{:S(2)}) collective-permute-start(bf16[128,1024]{1,0:T(8,128)(2,1)S(1)} %get-tuple-element.31), channel_id=1, source_target_pairs={{0,8},{8,0},{1,9},{9,1},{2,10},{10,2},{3,11},{11,3},{4,12},{12,4},... | collective-permute-start | bytes 786440 | tf_op jit(solution)/shard_map/grad_in/ppermute | solution.py:146
  147.5 4.8 %collective-permute-start.8 = (bf16[256,2048]{1,0:T(8,128)(2,1)}, bf16[256,2048]{1,0:T(8,128)(2,1)S(1)}, u32[]{:S(2)}, u32[]{:S(2)}) collective-permute-start(bf16[256,2048]{1,0:T(8,128)(2,1)} %bitcast.8), channel_id=1, source_target_pairs={{0,8},{8,0},{1,9},{9,1},{2,10},{10,2},{3,11},{11,3},{4,12},{12,4},... | collective-permute-start | bytes 3145736 | tf_op jit(solution)/shard_map/update/ppermute | solution.py:146

commit v3 on v2

--- a/solution.py
+++ b/solution.py
@@ -29,7 +29,7 @@
     return jax.ShapeDtypeStruct(dims, dtype)
 
 
-def call(body, outs, *args, first=None, cost=LONG):
+def call(body, outs, *args, first=None, cost=LONG, scratch=()):
     specs = [VMEM] * len(args)
     if first is not None:
         args, specs = (first,) + args, [ANY] + specs
@@ -39,8 +39,45 @@
         in_specs=specs,
         out_specs=(VMEM,) * len(outs) if isinstance(outs, tuple) else VMEM,
         compiler_params=pltpu.CompilerParams(vmem_limit_bytes=32 << 20),
+        scratch_shapes=scratch,
         cost_estimate=cost,
     )(*args)
+
+
+def picked(basis, core):
+    col = lax.broadcasted_iota(jnp.int32, (1, 256), 1)
+    z, x, yh, yl = col % 16, (col // 16) % 4, (col // 64) % 2, col // 128
+    want = (((yl * 16 + z) * 2 + core) * 2 + yh) * 4 + x
+    row = lax.broadcasted_iota(jnp.int32, (RANK, 256), 0)
+    pick = jnp.where(row == want, 1.0, 0.0).astype(bf16)
+    return jnp.dot(basis, pick, preferred_element_type=f32).astype(bf16)
+
+
+def pick_own_kernel(basis_ref, own_ref, sent_ref):
+    own = picked(basis_ref[...], lax.axis_index("c"))
+    own_ref[...] = own
+    for k in range(8):
+        sent_ref[k] = own
+
+
+def pick_other_kernel(_, basis_ref, out_ref):
+    out_ref[...] = picked(basis_ref[...], 1 - lax.axis_index("c"))
+
+
+def update_own_kernel(basis_ref, rows_ref, out_ref):
+    for k in range(4):
+        at = pl.ds(k * 512, 512)
+        out_ref[:, at] = jnp.dot(
+            basis_ref[...], rows_ref[:, at], preferred_element_type=f32
+        )
+
+
+def update_kernel(own_ref, basis_ref, rows_ref, out_ref):
+    at = pl.ds(pl.multiple_of(pl.program_id(0) * 512, 512), 512)
+    update = own_ref[:, at] + jnp.dot(
+        basis_ref[...], rows_ref[:, at], preferred_element_type=f32
+    )
+    out_ref[...] = (0.25 * update).astype(bf16)
 
 
 def half_kernel(_, w_ref, o_ref):
@@ -58,18 +95,36 @@
     upper_ref[...] = b_ref[128:]
 
 
-def backward_kernel(_, grad_ref, other_ref, pair, left, right, lower, upper, here, there):
+def blocks_of(refs, places):
     y, x = lax.axis_index("yh"), lax.axis_index("x")
-    blocks = [(pair, 0, 0, 0), (pair, 1, 1, 0), (left, 0, 0, 3), (left, 1, 1, 3)]
-    blocks += [(right, 0, 0, 1), (right, 1, 1, 1), (lower, 0, 0, 2), (upper, 0, 1, 2)]
-    for ref, part, dy, dx in blocks:
+    for ref, dy, dx in zip(refs, *places, strict=True):
         block = ((y + dy) % 2) * 4 + (x + dx) % 4
-        at = pl.ds(pl.multiple_of(block * 128, 128), 128)
-        w = ref[part * 128 : part * 128 + 128]
-        for g_ref, o_ref in ((grad_ref, here), (other_ref, there)):
+        yield pl.ds(pl.multiple_of(block * 128, 128), 128), ref
+
+
+NEAR = ((0, 1, 0, 1, 0, 1), (0, 0, 3, 3, 1, 1))
+FAR = ((0, 1), (2, 2))
+
+
+def multiply(pairs, blocks):
+    for at, ref in blocks:
+        w = ref[...]
+        for g_ref, o_ref in pairs:
             o_ref[:, at] = lax.dot_general(
                 g_ref[...], w, (((1,), (1,)), ((), ())), preferred_element_type=f32
             ).astype(bf16)
+
+
+def near_kernel(_, grad_ref, other_ref, pair, left, right, here, there):
+    refs = [r.at[pl.ds(k * 128, 128)] for r in (pair, left, right) for k in range(2)]
+    multiply(((grad_ref, here), (other_ref, there)), blocks_of(refs, NEAR))
+
+
+def far_kernel(near_here, near_there, grad_ref, other_ref, lower, upper, here, there):
+    for at, _ in blocks_of((None,) * 6, NEAR):
+        here[:, at] = near_here[:, at]
+        there[:, at] = near_there[:, at]
+    multiply(((grad_ref, here), (other_ref, there)), blocks_of((lower, upper), FAR))
 
 
 def weave_kernel(here_ref, there_ref, out_ref):
@@ -96,13 +151,12 @@
     m, v = m_ref[...], v_ref[...]
     p_ref[...] = p
     for k in range(16):
-        out_ref[k, :16] = p
-        out_ref[k, 16:32] = m
-        out_ref[k, 32:] = v
+        for t, row in enumerate((p, m, v)):
+            out_ref[k, 16 * t : 16 * t + 16] = row.astype(bf16)
 
 
 def squares_kernel(rows_ref, out_ref):
-    p = rows_ref[:, :16]
+    p = rows_ref[:, :16].astype(f32)
     out_ref[...] = jnp.full((32, 128), jnp.sum(p * p), f32)
 
 
@@ -113,23 +167,20 @@
     return first_new, second_new
 
 
-def adam_kernel(sums_ref, rows_ref, p_ref, m_ref, v_ref, out_ref, first_ref, second_ref):
+def adam_kernel(sums_ref, rows_ref, p_ref, m_ref, v_ref, out_ref, first_ref, second_ref, wide_ref):
     total = jnp.sum(sums_ref[...], 0, keepdims=True)
     limit = math.sqrt(RANK * D_OUT)
     factor = jnp.minimum(1.0, limit / (jnp.sqrt(total) + 1e-06))
     first_ref[...], second_ref[...] = adam(p_ref[...], m_ref[...], v_ref[...], factor)
+    wide_ref[...] = rows_ref[...].astype(f32)
     for j in range(16):
-        p, m, v = (rows_ref[:, 16 * t + j, :] for t in range(3))
+        p, m, v = (wide_ref[:, 16 * t + j, :] for t in range(3))
         f, s = adam(p, m, v, factor)
         d = (f / first_bias / (jnp.sqrt(s / second_bias) + 1e-08)).astype(bf16)
         for k in range(16):
             out_ref[k, :, pl.ds(j * 128, 128)] = d
 
 
-def spread(a, axes, peers):
-    return exchange(jnp.broadcast_to(a[None], (peers,) + a.shape), axes)
-
-
 def exchange(a, axes):
     return lax.all_to_all(a, axes, 0, 0, tiled=True)
 
@@ -146,23 +197,21 @@
         return lax.ppermute(a, "c", swap)
 
     with jax.named_scope("pick"):
-        col = lax.broadcasted_iota(jnp.int32, (RANK, RANK), 1)
-        row = lax.broadcasted_iota(jnp.int32, (RANK, RANK), 0)
-        own = jnp.where(col < 256, core, 1 - core)
-        z, x, yh, yl = col % 16, (col // 16) % 4, (col // 64) % 2, (col // 128) % 2
-        pick = (row == (((yl * 16 + z) * 2 + own) * 2 + yh) * 4 + x).astype(bf16)
-        basis_p = jnp.dot(basis, pick, preferred_element_type=f32).astype(bf16)
+        basis_own, basis_sent = call(
+            pick_own_kernel, (shape(256, 256), shape(8, 256, 256)), basis
+        )
     with jax.named_scope("swap_tokens"):
         grad_other = other(grad_out)
         acts2 = jnp.concatenate([acts, other(acts)], 0)
         grad2 = jnp.concatenate([grad_out, grad_other], 0)
     with jax.named_scope("basis"):
-        basis_all = spread(basis_p[:, :256], FSDP, 8).reshape(2048, 256)
+        basis_all = exchange(basis_sent, FSDP).reshape(2048, 256)
     with jax.named_scope("projected"):
         coords = jnp.dot(acts2, basis_all, preferred_element_type=f32).astype(bf16)
         part = lax.dot_general(
             coords, grad2, (((0,), (0,)), ((), ())), preferred_element_type=f32
         ).astype(bf16)
+        basis_other = call(pick_other_kernel, shape(256, 256), basis, first=part)
     with jax.named_scope("weight_y"):
         half = call(half_kernel, shape(128, 2048), weight, first=part)
         cross = lax.ppermute(half, "yh", swap)
@@ -181,29 +230,33 @@
     with jax.named_scope("rows_z"):
         p, rows = call(
             sum_z_kernel,
-            (shape(16, 128, dtype=f32), shape(16, 48, 128, dtype=f32)),
+            (shape(16, 128, dtype=f32), shape(16, 48, 128)),
             part, m, v,
         )
-    with jax.named_scope("weight_far"):
-        low, high = call(cut_kernel, (shape(128, 2048),) * 2, left, right, first=p)
-        lower, upper = shift(low, 1), shift(high, 3)
     with jax.named_scope("rows_z"):
         rows = exchange(rows, "z")
-        rows, low, high = lax.optimization_barrier((rows, low, high))
     with jax.named_scope("total"):
-        sums = exchange(call(squares_kernel, shape(32, 128, dtype=f32), rows), ("yl", "c", "yh", "x"))
+        sums = call(squares_kernel, shape(32, 128, dtype=f32), rows, cost=SHORT)
+    with jax.named_scope("weight_far"):
+        low, high = call(cut_kernel, (shape(128, 2048),) * 2, left, right, first=sums, cost=SHORT)
+        lower, upper = shift(low, 1), shift(high, 3)
+    with jax.named_scope("total"):
+        sums = exchange(sums, ("yl", "c", "yh", "x"))
+        sums, low, high = lax.optimization_barrier((sums, low, high))
     with jax.named_scope("adam"):
         direction, first_new, second_new = call(
             adam_kernel,
             (shape(16, 16, D_OUT), shape(16, 128, dtype=f32), shape(16, 128, dtype=f32)),
             sums, rows, p, m, v,
+            scratch=[pltpu.VMEM((16, 48, 128), f32)],
         )
     with jax.named_scope("grad_in"):
+        out = (shape(128, 1024),) * 2
+        near = call(
+            near_kernel, out, grad_out, grad_other, pair, left, right, first=direction
+        )
         here, there = call(
-            backward_kernel,
-            (shape(128, 1024),) * 2,
-            grad_out, grad_other, pair, left, right, lower, upper,
-            first=direction,
+            far_kernel, out, *near, grad_out, grad_other, lower, upper, cost=SHORT
         )
         grad_in = call(weave_kernel, shape(128, D_OUT), here, other(there), cost=SHORT)
     with jax.named_scope("rows_yx"):
@@ -211,9 +264,16 @@
         mine, grad_in = lax.optimization_barrier((mine, grad_in))
     with jax.named_scope("update"):
         theirs = other(mine)
-        update = jnp.dot(basis_p[:, :256], mine, preferred_element_type=f32)
-        update = update + jnp.dot(basis_p[:, 256:], theirs, preferred_element_type=f32)
-        weight_update = (0.25 * update).astype(bf16)
+        update = call(update_own_kernel, shape(256, D_OUT, dtype=f32), basis_own, mine)
+        weight_update = pl.pallas_call(
+            update_kernel,
+            out_shape=shape(256, D_OUT),
+            grid=(4,),
+            in_specs=[VMEM] * 3,
+            out_specs=pl.BlockSpec((256, 512), lambda i: (0, i)),
+            compiler_params=pltpu.CompilerParams(vmem_limit_bytes=32 << 20),
+            cost_estimate=SHORT,
+        )(update, basis_other, theirs)
     return (
         grad_in,
         first_new.reshape(1, D_OUT),

time: 157 us -> 149 us (0.949)
  blocking collectives: 0 us -> 18 us
  waiting for transfers between devices: 49.2 us -> 31.5 us
  starting transfers between devices: 83.9 us -> 74.1 us
  matrix products: 5.87 us -> 2.36 us
  Pallas kernels: 10.1 us -> 12.7 us
  local copies, waits for them, and re-layouts: 5.38 us -> 7.56 us
    all_to_all x0 -> x1, blocking collectives: none -> 18 us  [exchange(): return lax.all_to_all(a, axes, 0, 0, tiled=True)]
    ppermute x4, waiting for transfers between devices: 13.8 us -> 0.01 us  [shift(): return lax.ppermute(a, 'x', [(i, (i + k) % 4) for i in range(4)])]
    all_to_all x6 -> x5, starting transfers between devices: 51.3 us -> 41.9 us  [exchange(): return lax.all_to_all(a, axes, 0, 0, tiled=True)]
    dot_general x3 -> x0, matrix products: 3.51 us -> none  [the longest x1 2.68 us: on_device(): update = jnp.dot(basis_p[:, :256], mine, preferred_element_type=f32)]
    unnamed x24 -> x36, local copies, waits for them, and re-layouts: 4.24 us -> 7.56 us
    all_to_all x6 -> x5, waiting for transfers between devices: 29.9 us -> 26.9 us  [exchange(): return lax.all_to_all(a, axes, 0, 0, tiled=True)]
    pallas_call x0 -> x1, Pallas kernels: none -> 2.12 us  [on_device(): pl.pallas_call(update_kernel, out_shape=shape(256, D_OUT), grid=(4,), in_...]
    pallas_call x9 -> x13, Pallas kernels: 10.1 us -> 10.6 us  [call(): pl.pallas_call(body, out_shape=outs, in_specs=specs, out_specs=(VMEM,) *...]
  transfers between devices with their start and end apart: 15 -> 14, of which waited for: 12 -> 7; matrix products, arithmetic and copies ran while one was open for 0% -> 0% of each run, Pallas kernels for 6% -> 6%
where the time goes in v3:
time: 149 us; the launch traced here: 147 us
  starting transfers between devices  74.1 us (50%)
  waiting for transfers between devices  31.5 us (21%)
  blocking collectives  18 us (12%)
  Pallas kernels  12.7 us (9%)
  local copies, waits for them, and re-layouts  7.56 us (5%)
  matrix products  2.36 us (2%)
    all_to_all x5, starting transfers between devices, exchange(): return lax.all_to_all(a, axes, 0, 0, tiled=True)  41.9 us
    all_to_all x5, waiting for transfers between devices, exchange(): return lax.all_to_all(a, axes, 0, 0, tiled=True)  26.9 us
    all_to_all x1, blocking collectives, exchange(): return lax.all_to_all(a, axes, 0, 0, tiled=True)  18 us
    ppermute x4, starting transfers between devices, other(): return lax.ppermute(a, 'c', swap)  15.7 us
    ppermute x4, starting transfers between devices, shift(): return lax.ppermute(a, 'x', [(i, (i + k) % 4) for i in range(4)])  11.8 us
    pallas_call x13, Pallas kernels, call(): pl.pallas_call(body, out_shape=outs, in_specs=specs, out_specs=(VMEM,) *...  10.6 us
    unnamed x36, local copies, waits for them, and re-layouts  7.56 us
    ppermute x1, starting transfers between devices, on_device(): cross = lax.ppermute(half, 'yh', swap)  4.67 us
  transfers between devices with their start and end apart: 14, of which 7 were waited for; matrix products, arithmetic and copies ran while one was open for 0% of the time, Pallas kernels for 6%

profile of v3, /device:TPU:1, one launch (start us, length us, event | category | flops | bytes accessed | tf_op | source)
XLA Modules:
  0.0 147.1 jit_solution(2275286971276787538)
XLA Ops:
  1.6 1.2 pick.1
  2.8 7.6 %all-to-all-start = ((bf16[8,256,256]{2,1,0:T(8,128)(2,1)}), bf16[8,256,256]{2,1,0:T(8,128)(2,1)S(1)}, u32[]{:S(2)}, u32[]{:S(2)}) async-start(bf16[8,256,256]{2,1,0:T(8,128)(2,1)} %get-tuple-element.24), calls=%async_computation | async-start | bytes 2097152 | tf_op jit(solution)/shard_map/basis/all_to_all | solution.py:185
  10.4 4.9 %collective-permute-start = (bf16[128,2048]{1,0:T(8,128)(2,1)S(1)}, bf16[128,2048]{1,0:T(8,128)(2,1)S(1)}, u32[]{:S(2)}, u32[]{:S(2)}) collective-permute-start(bf16[128,2048]{1,0:T(8,128)(2,1)S(1)} %copy-done.17), channel_id=1, source_target_pairs={{0,8},{8,0},{1,9},{9,1},{2,10},{10,2},{3,11},{11,3},{4,12},{12,4},... | collective-permute-start | bytes 1572872 | tf_op jit(solution)/shard_map/swap_tokens/ppermute | solution.py:197
  15.3 1.9 %collective-permute-start.1 = (bf16[128,2048]{1,0:T(8,128)(2,1)S(1)}, bf16[128,2048]{1,0:T(8,128)(2,1)S(1)}, u32[]{:S(2)}, u32[]{:S(2)}) collective-permute-start(bf16[128,2048]{1,0:T(8,128)(2,1)S(1)} %copy-done.2), channel_id=1, source_target_pairs={{0,8},{8,0},{1,9},{9,1},{2,10},{10,2},{3,11},{11,3},{4,12},{12,4},... | collective-permute-start | bytes 1572872 | tf_op jit(solution)/shard_map/swap_tokens/ppermute | solution.py:197
  17.3 1.9 %collective-permute-done.1.other_ref = bf16[128,2048]{1,0:T(8,128)(2,1)S(1)} collective-permute-done((bf16[128,2048]{1,0:T(8,128)(2,1)S(1)}, bf16[128,2048]{1,0:T(8,128)(2,1)S(1)}, u32[]{:S(2)}, u32[]{:S(2)}) %collective-permute-start.1) | collective-permute-done | bytes 524320 | tf_op jit(solution)/shard_map/swap_tokens/ppermute | solution.py:197
  19.1 8.5 %all-to-all-done = bf16[8,256,256]{2,1,0:T(8,128)(2,1)S(1)} async-done(((bf16[8,256,256]{2,1,0:T(8,128)(2,1)}), bf16[8,256,256]{2,1,0:T(8,128)(2,1)S(1)}, u32[]{:S(2)}, u32[]{:S(2)}) %all-to-all-start) | async-done | bytes 1048608 | tf_op jit(solution)/shard_map/basis/all_to_all | solution.py:185
  27.6 2.4 %convolution_convert_fusion._ = bf16[256,2048]{1,0:T(8,128)(2,1)} fusion(bf16[2048,256]{1,0:T(8,128)(2,1)S(1)} %bitcast.19, bf16[128,2048]{1,0:T(8,128)(2,1)S(1)} %collective-permute-done, bf16[128,2048]{1,0:T(8,128)(2,1)S(1)} %copy-done.17, bf16[128,2048]{1,0:T(8,128)(2,1)S(1)} %collective-permute-done.1.other_ref, bf16[128,2048]{1,0:T(8,128)(2,1)S(1)} %copy-done.2), kind=kOutput, calls=%fused_computation | convolution fusion | flops 541655040 | bytes 4194304 | tf_op jit(solution)/shard_map/projected/dot_general | solution.py:211
  30.0 3.8 %all-to-all-start.1 = ((bf16[16,16,2048]{2,1,0:T(8,128)(2,1)}), bf16[16,16,2048]{2,1,0:T(8,128)(2,1)S(1)}, u32[]{:S(2)}, u32[]{:S(2)}) async-start(bf16[16,16,2048]{2,1,0:T(8,128)(2,1)} %bitcast.1), calls=%async_computation.1 | async-start | bytes 2097152 | tf_op jit(solution)/shard_map/sum_yx/all_to_all | solution.py:185
  33.9 4.7 %collective-permute-start.2 = (bf16[128,2048]{1,0:T(8,128)(2,1)S(1)}, bf16[128,2048]{1,0:T(8,128)(2,1)S(1)}, u32[]{:S(2)}, u32[]{:S(2)}) collective-permute-start(bf16[128,2048]{1,0:T(8,128)(2,1)S(1)} %weight_y.1.a_ref), channel_id=1, source_target_pairs={{0,4},{4,0},{1,5},{5,1},{2,6},{6,2},{3,7},{7,3},{8,12},{12,8},{9,1... | collective-permute-start | bytes 1572872 | tf_op jit(solution)/shard_map/weight_y/ppermute | solution.py:217
  38.5 11.8 %all-to-all-done.1.in_ref = bf16[16,16,2048]{2,1,0:T(8,128)(2,1)S(1)} async-done(((bf16[16,16,2048]{2,1,0:T(8,128)(2,1)}), bf16[16,16,2048]{2,1,0:T(8,128)(2,1)S(1)}, u32[]{:S(2)}, u32[]{:S(2)}) %all-to-all-start.1) | async-done | bytes 1048608 | tf_op jit(solution)/shard_map/sum_yx/all_to_all | solution.py:185
  51.2 15.3 %all-to-all-start.2 = ((f32[16,16,128]{2,1,0:T(8,128)}), f32[16,16,128]{2,1,0:T(8,128)S(1)}, u32[]{:S(2)}, u32[]{:S(2)}) async-start(f32[16,16,128]{2,1,0:T(8,128)} %sum_yx.1._), calls=%async_computation.2 | async-start | bytes 262144 | tf_op jit(solution)/shard_map/sum_z/all_to_all | solution.py:185
  66.5 1.0 copy-done.12
  67.6 1.9 %collective-permute-start.4 = (bf16[256,2048]{1,0:T(8,128)(2,1)S(1)}, bf16[256,2048]{1,0:T(8,128)(2,1)S(1)}, u32[]{:S(2)}, u32[]{:S(2)}) collective-permute-start(bf16[256,2048]{1,0:T(8,128)(2,1)S(1)} %weight_x.1.pair), channel_id=1, source_target_pairs={{0,3},{1,0},{2,1},{3,2},{4,7},{5,4},{6,5},{7,6},{8,11},{9,8},{10,9... | collective-permute-start | bytes 3145736 | tf_op jit(solution)/shard_map/weight_x/ppermute | solution.py:189
  69.5 3.4 %collective-permute-start.3 = (bf16[256,2048]{1,0:T(8,128)(2,1)S(1)}, bf16[256,2048]{1,0:T(8,128)(2,1)S(1)}, u32[]{:S(2)}, u32[]{:S(2)}) collective-permute-start(bf16[256,2048]{1,0:T(8,128)(2,1)S(1)} %weight_x.1.pair), channel_id=1, source_target_pairs={{0,1},{1,2},{2,3},{3,0},{4,5},{5,6},{6,7},{7,4},{8,9},{9,10},{10,1... | collective-permute-start | bytes 3145736 | tf_op jit(solution)/shard_map/weight_x/ppermute | solution.py:189
  72.9 5.6 %all-to-all-done.2.in_ref = f32[16,16,128]{2,1,0:T(8,128)S(1)} async-done(((f32[16,16,128]{2,1,0:T(8,128)}), f32[16,16,128]{2,1,0:T(8,128)S(1)}, u32[]{:S(2)}, u32[]{:S(2)}) %all-to-all-start.2) | async-done | bytes 131104 | tf_op jit(solution)/shard_map/sum_z/all_to_all | solution.py:185
  78.6 18.0 %all_to_all.37.rows_ref = bf16[16,48,128]{2,1,0:T(8,128)(2,1)S(1)} all-to-all(bf16[16,48,128]{2,1,0:T(8,128)(2,1)S(1)} %get-tuple-element.28), channel_id=1, replica_groups=mesh['yl'=2,'z'=16,'c'=2,'yh'=2,'x'=4] {'z'}, dimensions={0} | all-to-all | bytes 393216 | tf_op jit(solution)/shard_map/rows_z/all_to_all | solution.py:185
  97.3 9.8 %all-to-all-start.4 = ((f32[32,1,128]{2,1,0:T(1,128)}), f32[32,1,128]{2,1,0:T(1,128)S(1)}, u32[]{:S(2)}, u32[]{:S(2)}) async-start(f32[32,1,128]{2,1,0:T(1,128)} %bitcast.5), calls=%async_computation.4 | async-start | bytes 32768 | tf_op jit(solution)/shard_map/total/all_to_all | solution.py:185
  107.1 1.1 weight_far.1
  108.2 3.3 %collective-permute-start.5 = (bf16[128,2048]{1,0:T(8,128)(2,1)}, bf16[128,2048]{1,0:T(8,128)(2,1)}, u32[]{:S(2)}, u32[]{:S(2)}) collective-permute-start(bf16[128,2048]{1,0:T(8,128)(2,1)} %get-tuple-element.29), channel_id=1, source_target_pairs={{0,1},{1,2},{2,3},{3,0},{4,5},{5,6},{6,7},{7,4},{8,9},{9,10},{10,1... | collective-permute-start | bytes 1572872 | tf_op jit(solution)/shard_map/weight_far/ppermute | solution.py:189
  111.5 3.2 %collective-permute-start.6 = (bf16[128,2048]{1,0:T(8,128)(2,1)}, bf16[128,2048]{1,0:T(8,128)(2,1)}, u32[]{:S(2)}, u32[]{:S(2)}) collective-permute-start(bf16[128,2048]{1,0:T(8,128)(2,1)} %get-tuple-element.30), channel_id=1, source_target_pairs={{0,3},{1,0},{2,1},{3,2},{4,7},{5,4},{6,5},{7,6},{8,11},{9,8},{10,9... | collective-permute-start | bytes 1572872 | tf_op jit(solution)/shard_map/weight_far/ppermute | solution.py:189
  114.7 1.1 adam.1
  116.8 5.5 %all-to-all-start.5 = ((bf16[16,16,2048]{2,1,0:T(8,128)(2,1)}), bf16[16,16,2048]{2,1,0:T(8,128)(2,1)S(1)}, u32[]{:S(2)}, u32[]{:S(2)}) async-start(bf16[16,16,2048]{2,1,0:T(8,128)(2,1)} %copy-done), calls=%async_computation.5 | async-start | bytes 2097152 | tf_op jit(solution)/shard_map/rows_yx/all_to_all | solution.py:185
  122.3 1.2 copy-done.1
  123.6 1.0 copy-done.3
  124.6 1.0 copy-done.6
  125.6 1.2 copy-done.10
  126.9 1.8 %grad_in.3 = (bf16[128,1024]{1,0:T(8,128)(2,1)S(1)}, bf16[128,1024]{1,0:T(8,128)(2,1)S(1)}) custom-call(bf16[16,16,2048]{2,1,0:T(8,128)(2,1)S(1)} %copy-done.1, bf16[128,2048]{1,0:T(8,128)(2,1)S(1)} %copy-done.3, bf16[128,2048]{1,0:T(8,128)(2,1)S(1)} %copy-done.6, bf16[256,2048]{1,0:T(8,128)(2,1)S(1)} %copy-done.10, ...), custom_call_target="tpu_custom_call" | custom-call | flops 20000000000 | bytes 1048576 | tf_op jit(solution)/shard_map/grad_in/pallas_call | solution.py:36
  128.7 2.0 %grad_in.4 = (bf16[128,1024]{1,0:T(8,128)(2,1)S(1)}, bf16[128,1024]{1,0:T(8,128)(2,1)S(1)}) custom-call(bf16[128,1024]{1,0:T(8,128)(2,1)S(1)} %get-tuple-element.35.near_here, bf16[128,1024]{1,0:T(8,128)(2,1)S(1)} %get-tuple-element.36.near_there, bf16[128,2048]{1,0:T(8,128)(2,1)S(1)} %copy-done.4, bf16[128,2048]{1,0:T(8,128)(2,1)S(1)} %copy-done.7, ...), custom_call_target="tpu_custom_call" | custom-call | flops 1000 | bytes 1000 | tf_op jit(solution)/shard_map/grad_in/pallas_call | solution.py:36
  130.7 4.9 %collective-permute-start.7 = (bf16[128,1024]{1,0:T(8,128)(2,1)S(1)}, bf16[128,1024]{1,0:T(8,128)(2,1)S(1)}, u32[]{:S(2)}, u32[]{:S(2)}) collective-permute-start(bf16[128,1024]{1,0:T(8,128)(2,1)S(1)} %get-tuple-element.38), channel_id=1, source_target_pairs={{0,8},{8,0},{1,9},{9,1},{2,10},{10,2},{3,11},{11,3},{4,12},{12,4},... | collective-permute-start | bytes 786440 | tf_op jit(solution)/shard_map/grad_in/ppermute | solution.py:197
  138.7 4.0 %collective-permute-start.8 = (bf16[256,2048]{1,0:T(8,128)(2,1)S(1)}, bf16[256,2048]{1,0:T(8,128)(2,1)S(1)}, u32[]{:S(2)}, u32[]{:S(2)}) collective-permute-start(bf16[256,2048]{1,0:T(8,128)(2,1)S(1)} %bitcast.12), channel_id=1, source_target_pairs={{0,8},{8,0},{1,9},{9,1},{2,10},{10,2},{3,11},{11,3},{4,12},{12,4},... | collective-permute-start | bytes 3145736 | tf_op jit(solution)/shard_map/update/ppermute | solution.py:197
  143.2 1.8 %collective-permute-done.8.rows_ref = bf16[256,2048]{1,0:T(8,128)(2,1)S(1)} collective-permute-done((bf16[256,2048]{1,0:T(8,128)(2,1)S(1)}, bf16[256,2048]{1,0:T(8,128)(2,1)S(1)}, u32[]{:S(2)}, u32[]{:S(2)}) %collective-permute-start.8) | collective-permute-done | bytes 1048608 | tf_op jit(solution)/shard_map/update/ppermute | solution.py:197
  145.0 2.1 %update.3 = bf16[256,2048]{1,0:T(8,128)(2,1)} custom-call(f32[256,2048]{1,0:T(8,128)S(1)} %update.2.own_ref, bf16[256,256]{1,0:T(8,128)(2,1)S(1)} %projected.1.basis_ref, bf16[256,2048]{1,0:T(8,128)(2,1)S(1)} %collective-permute-done.8.rows_ref), custom_call_target="tpu_custom_call" | custom-call | flops 1000 | bytes 1000 | tf_op jit(solution)/shard_map/update/pallas_call | solution.py:268
  (48 shorter events, 7.2 us)
Async XLA Ops:
  0.6 1.0 copy-start.13
  2.8 7.6 %copy-start.17 = (bf16[128,2048]{1,0:T(8,128)(2,1)S(1)}, bf16[128,2048]{1,0:T(8,128)(2,1)}, u32[]{:S(2)}) copy-start(bf16[128,2048]{1,0:T(8,128)(2,1)} %param.6) | copy-start | bytes 1572868
  2.8 12.5 %copy-start.2 = (bf16[128,2048]{1,0:T(8,128)(2,1)S(1)}, bf16[128,2048]{1,0:T(8,128)(2,1)}, u32[]{:S(2)}) copy-start(bf16[128,2048]{1,0:T(8,128)(2,1)} %grad_ref.3) | copy-start | bytes 1572868
  2.8 24.8 %all-to-all-start = ((bf16[8,256,256]{2,1,0:T(8,128)(2,1)}), bf16[8,256,256]{2,1,0:T(8,128)(2,1)S(1)}, u32[]{:S(2)}, u32[]{:S(2)}) async-start(bf16[8,256,256]{2,1,0:T(8,128)(2,1)} %get-tuple-element.24), calls=%async_computation | async-start | bytes 2097152 | tf_op jit(solution)/shard_map/basis/all_to_all | solution.py:185
  10.4 6.8 %collective-permute-start = (bf16[128,2048]{1,0:T(8,128)(2,1)S(1)}, bf16[128,2048]{1,0:T(8,128)(2,1)S(1)}, u32[]{:S(2)}, u32[]{:S(2)}) collective-permute-start(bf16[128,2048]{1,0:T(8,128)(2,1)S(1)} %copy-done.17), channel_id=1, source_target_pairs={{0,8},{8,0},{1,9},{9,1},{2,10},{10,2},{3,11},{11,3},{4,12},{12,4},... | collective-permute-start | bytes 1572872 | tf_op jit(solution)/shard_map/swap_tokens/ppermute | solution.py:197
  15.3 3.8 %collective-permute-start.1 = (bf16[128,2048]{1,0:T(8,128)(2,1)S(1)}, bf16[128,2048]{1,0:T(8,128)(2,1)S(1)}, u32[]{:S(2)}, u32[]{:S(2)}) collective-permute-start(bf16[128,2048]{1,0:T(8,128)(2,1)S(1)} %copy-done.2), channel_id=1, source_target_pairs={{0,8},{8,0},{1,9},{9,1},{2,10},{10,2},{3,11},{11,3},{4,12},{12,4},... | collective-permute-start | bytes 1572872 | tf_op jit(solution)/shard_map/swap_tokens/ppermute | solution.py:197
  19.1 10.8 %copy-start.5 = (bf16[128,2048]{1,0:T(8,128)(2,1)}, bf16[128,2048]{1,0:T(8,128)(2,1)S(1)}, u32[]{:S(2)}) copy-start(bf16[128,2048]{1,0:T(8,128)(2,1)S(1)} %collective-permute-done.1.other_ref) | copy-start | bytes 1572868
  30.0 3.8 %copy-start.8 = (bf16[256,2048]{1,0:T(8,128)(2,1)S(1)}, bf16[256,2048]{1,0:T(8,128)(2,1)}, u32[]{:S(2)}) copy-start(bf16[256,2048]{1,0:T(8,128)(2,1)} %w_ref.1) | copy-start | bytes 3145732
  30.0 20.3 %all-to-all-start.1 = ((bf16[16,16,2048]{2,1,0:T(8,128)(2,1)}), bf16[16,16,2048]{2,1,0:T(8,128)(2,1)S(1)}, u32[]{:S(2)}, u32[]{:S(2)}) async-start(bf16[16,16,2048]{2,1,0:T(8,128)(2,1)} %bitcast.1), calls=%async_computation.1 | async-start | bytes 2097152 | tf_op jit(solution)/shard_map/sum_yx/all_to_all | solution.py:185
  33.8 17.3 %copy-start.11 = (bf16[128,2048]{1,0:T(8,128)(2,1)}, bf16[128,2048]{1,0:T(8,128)(2,1)S(1)}, u32[]{:S(2)}) copy-start(bf16[128,2048]{1,0:T(8,128)(2,1)S(1)} %weight_y.1.a_ref) | copy-start | bytes 1572868
  33.9 32.6 %collective-permute-start.2 = (bf16[128,2048]{1,0:T(8,128)(2,1)S(1)}, bf16[128,2048]{1,0:T(8,128)(2,1)S(1)}, u32[]{:S(2)}, u32[]{:S(2)}) collective-permute-start(bf16[128,2048]{1,0:T(8,128)(2,1)S(1)} %weight_y.1.a_ref), channel_id=1, source_target_pairs={{0,4},{4,0},{1,5},{5,1},{2,6},{6,2},{3,7},{7,3},{8,12},{12,8},{9,1... | collective-permute-start | bytes 1572872 | tf_op jit(solution)/shard_map/weight_y/ppermute | solution.py:217
  51.2 27.4 %all-to-all-start.2 = ((f32[16,16,128]{2,1,0:T(8,128)}), f32[16,16,128]{2,1,0:T(8,128)S(1)}, u32[]{:S(2)}, u32[]{:S(2)}) async-start(f32[16,16,128]{2,1,0:T(8,128)} %sum_yx.1._), calls=%async_computation.2 | async-start | bytes 262144 | tf_op jit(solution)/shard_map/sum_z/all_to_all | solution.py:185
  66.5 1.0 copy-start.12
  67.5 11.0 %copy-start.15 = (f32[1,2048]{1,0:T(1,128)S(1)}, f32[1,2048]{1,0:T(1,128)}, u32[]{:S(2)}) copy-start(f32[1,2048]{1,0:T(1,128)} %param.10) | copy-start | bytes 24580
  67.5 11.0 %copy-start.16 = (f32[1,2048]{1,0:T(1,128)S(1)}, f32[1,2048]{1,0:T(1,128)}, u32[]{:S(2)}) copy-start(f32[1,2048]{1,0:T(1,128)} %param.11) | copy-start | bytes 24580
  67.6 11.0 %copy-start.9 = (bf16[256,2048]{1,0:T(8,128)(2,1)}, bf16[256,2048]{1,0:T(8,128)(2,1)S(1)}, u32[]{:S(2)}) copy-start(bf16[256,2048]{1,0:T(8,128)(2,1)S(1)} %weight_x.1.pair) | copy-start | bytes 3145732
  67.6 39.5 %collective-permute-start.4 = (bf16[256,2048]{1,0:T(8,128)(2,1)S(1)}, bf16[256,2048]{1,0:T(8,128)(2,1)S(1)}, u32[]{:S(2)}, u32[]{:S(2)}) collective-permute-start(bf16[256,2048]{1,0:T(8,128)(2,1)S(1)} %weight_x.1.pair), channel_id=1, source_target_pairs={{0,3},{1,0},{2,1},{3,2},{4,7},{5,4},{6,5},{7,6},{8,11},{9,8},{10,9... | collective-permute-start | bytes 3145736 | tf_op jit(solution)/shard_map/weight_x/ppermute | solution.py:189
  69.5 37.6 %collective-permute-start.3 = (bf16[256,2048]{1,0:T(8,128)(2,1)S(1)}, bf16[256,2048]{1,0:T(8,128)(2,1)S(1)}, u32[]{:S(2)}, u32[]{:S(2)}) collective-permute-start(bf16[256,2048]{1,0:T(8,128)(2,1)S(1)} %weight_x.1.pair), channel_id=1, source_target_pairs={{0,1},{1,2},{2,3},{3,0},{4,5},{5,6},{6,7},{7,4},{8,9},{9,10},{10,1... | collective-permute-start | bytes 3145736 | tf_op jit(solution)/shard_map/weight_x/ppermute | solution.py:189
  97.3 17.4 %all-to-all-start.4 = ((f32[32,1,128]{2,1,0:T(1,128)}), f32[32,1,128]{2,1,0:T(1,128)S(1)}, u32[]{:S(2)}, u32[]{:S(2)}) async-start(f32[32,1,128]{2,1,0:T(1,128)} %bitcast.5), calls=%async_computation.4 | async-start | bytes 32768 | tf_op jit(solution)/shard_map/total/all_to_all | solution.py:185
  108.2 20.5 %collective-permute-start.5 = (bf16[128,2048]{1,0:T(8,128)(2,1)}, bf16[128,2048]{1,0:T(8,128)(2,1)}, u32[]{:S(2)}, u32[]{:S(2)}) collective-permute-start(bf16[128,2048]{1,0:T(8,128)(2,1)} %get-tuple-element.29), channel_id=1, source_target_pairs={{0,1},{1,2},{2,3},{3,0},{4,5},{5,6},{6,7},{7,4},{8,9},{9,10},{10,1... | collective-permute-start | bytes 1572872 | tf_op jit(solution)/shard_map/weight_far/ppermute | solution.py:189
  111.5 17.2 %collective-permute-start.6 = (bf16[128,2048]{1,0:T(8,128)(2,1)}, bf16[128,2048]{1,0:T(8,128)(2,1)}, u32[]{:S(2)}, u32[]{:S(2)}) collective-permute-start(bf16[128,2048]{1,0:T(8,128)(2,1)} %get-tuple-element.30), channel_id=1, source_target_pairs={{0,3},{1,0},{2,1},{3,2},{4,7},{5,4},{6,5},{7,6},{8,11},{9,8},{10,9... | collective-permute-start | bytes 1572872 | tf_op jit(solution)/shard_map/weight_far/ppermute | solution.py:189
  115.8 1.0 copy-start
  116.8 21.9 %all-to-all-start.5 = ((bf16[16,16,2048]{2,1,0:T(8,128)(2,1)}), bf16[16,16,2048]{2,1,0:T(8,128)(2,1)S(1)}, u32[]{:S(2)}, u32[]{:S(2)}) async-start(bf16[16,16,2048]{2,1,0:T(8,128)(2,1)} %copy-done), calls=%async_computation.5 | async-start | bytes 2097152 | tf_op jit(solution)/shard_map/rows_yx/all_to_all | solution.py:185
  122.3 1.3 copy-start.1
  123.5 1.0 copy-start.3
  124.6 1.0 copy-start.6
  125.6 1.2 copy-start.10
  126.9 1.8 %copy-start.4 = (bf16[128,2048]{1,0:T(8,128)(2,1)S(1)}, bf16[128,2048]{1,0:T(8,128)(2,1)}, u32[]{:S(2)}) copy-start(bf16[128,2048]{1,0:T(8,128)(2,1)} %grad_ref.3) | copy-start | bytes 1572868
  126.9 1.8 %copy-start.7 = (bf16[128,2048]{1,0:T(8,128)(2,1)S(1)}, bf16[128,2048]{1,0:T(8,128)(2,1)}, u32[]{:S(2)}) copy-start(bf16[128,2048]{1,0:T(8,128)(2,1)} %copy-done.5) | copy-start | bytes 1572868
  128.7 7.0 %copy-start.14 = (bf16[256,512]{1,0:T(8,128)(2,1)S(1)}, bf16[256,512]{1,0:T(8,128)(2,1)}, u32[]{:S(2)}) copy-start(bf16[256,512]{1,0:T(8,128)(2,1)} %basis_ref.3) | copy-start | bytes 786436
  130.7 6.1 %collective-permute-start.7 = (bf16[128,1024]{1,0:T(8,128)(2,1)S(1)}, bf16[128,1024]{1,0:T(8,128)(2,1)S(1)}, u32[]{:S(2)}, u32[]{:S(2)}) collective-permute-start(bf16[128,1024]{1,0:T(8,128)(2,1)S(1)} %get-tuple-element.38), channel_id=1, source_target_pairs={{0,8},{8,0},{1,9},{9,1},{2,10},{10,2},{3,11},{11,3},{4,12},{12,4},... | collective-permute-start | bytes 786440 | tf_op jit(solution)/shard_map/grad_in/ppermute | solution.py:197
  138.7 6.3 %collective-permute-start.8 = (bf16[256,2048]{1,0:T(8,128)(2,1)S(1)}, bf16[256,2048]{1,0:T(8,128)(2,1)S(1)}, u32[]{:S(2)}, u32[]{:S(2)}) collective-permute-start(bf16[256,2048]{1,0:T(8,128)(2,1)S(1)} %bitcast.12), channel_id=1, source_target_pairs={{0,8},{8,0},{1,9},{9,1},{2,10},{10,2},{3,11},{11,3},{4,12},{12,4},... | collective-permute-start | bytes 3145736 | tf_op jit(solution)/shard_map/update/ppermute | solution.py:197

commit v4 on v3

--- a/solution.py
+++ b/solution.py
@@ -73,7 +73,7 @@
 
 
 def update_kernel(own_ref, basis_ref, rows_ref, out_ref):
-    at = pl.ds(pl.multiple_of(pl.program_id(0) * 512, 512), 512)
+    at = pl.ds(pl.multiple_of(pl.program_id(0) * 1024, 1024), 1024)
     update = own_ref[:, at] + jnp.dot(
         basis_ref[...], rows_ref[:, at], preferred_element_type=f32
     )
@@ -90,9 +90,14 @@
     o_ref[128:] = b_ref[...]
 
 
-def cut_kernel(_, a_ref, b_ref, lower_ref, upper_ref):
-    lower_ref[...] = a_ref[:128]
-    upper_ref[...] = b_ref[128:]
+def choose_kernel(_, left_ref, right_ref, out_ref):
+    @pl.when(lax.axis_index("c") == 0)
+    def _():
+        out_ref[...] = left_ref[...]
+
+    @pl.when(lax.axis_index("c") == 1)
+    def _():
+        out_ref[...] = right_ref[...]
 
 
 def blocks_of(refs, places):
@@ -100,6 +105,10 @@
     for ref, dy, dx in zip(refs, *places, strict=True):
         block = ((y + dy) % 2) * 4 + (x + dx) % 4
         yield pl.ds(pl.multiple_of(block * 128, 128), 128), ref
+
+
+def halves(ref):
+    return [ref.at[pl.ds(k * 128, 128)] for k in range(2)]
 
 
 NEAR = ((0, 1, 0, 1, 0, 1), (0, 0, 3, 3, 1, 1))
@@ -116,15 +125,15 @@
 
 
 def near_kernel(_, grad_ref, other_ref, pair, left, right, here, there):
-    refs = [r.at[pl.ds(k * 128, 128)] for r in (pair, left, right) for k in range(2)]
+    refs = halves(pair) + halves(left) + halves(right)
     multiply(((grad_ref, here), (other_ref, there)), blocks_of(refs, NEAR))
 
 
-def far_kernel(near_here, near_there, grad_ref, other_ref, lower, upper, here, there):
+def far_kernel(near_here, near_there, grad_ref, other_ref, far, here, there):
     for at, _ in blocks_of((None,) * 6, NEAR):
         here[:, at] = near_here[:, at]
         there[:, at] = near_there[:, at]
-    multiply(((grad_ref, here), (other_ref, there)), blocks_of((lower, upper), FAR))
+    multiply(((grad_ref, here), (other_ref, there)), blocks_of(halves(far), FAR))
 
 
 def weave_kernel(here_ref, there_ref, out_ref):
@@ -238,11 +247,13 @@
     with jax.named_scope("total"):
         sums = call(squares_kernel, shape(32, 128, dtype=f32), rows, cost=SHORT)
     with jax.named_scope("weight_far"):
-        low, high = call(cut_kernel, (shape(128, 2048),) * 2, left, right, first=sums, cost=SHORT)
-        lower, upper = shift(low, 1), shift(high, 3)
+        passed = call(choose_kernel, shape(256, 2048), left, right, first=sums, cost=SHORT)
+        onward = [(i, (i + 1) % 4) for i in range(4)]
+        onward += [(4 + i, 4 + (i + 3) % 4) for i in range(4)]
+        far = lax.ppermute(passed, ("c", "x"), onward)
     with jax.named_scope("total"):
         sums = exchange(sums, ("yl", "c", "yh", "x"))
-        sums, low, high = lax.optimization_barrier((sums, low, high))
+        sums, passed = lax.optimization_barrier((sums, passed))
     with jax.named_scope("adam"):
         direction, first_new, second_new = call(
             adam_kernel,
@@ -253,10 +264,10 @@
     with jax.named_scope("grad_in"):
         out = (shape(128, 1024),) * 2
         near = call(
-            near_kernel, out, grad_out, grad_other, pair, left, right, first=direction
+            near_kernel, out, grad_out, grad_other, pair, left, right, first=first_new
         )
         here, there = call(
-            far_kernel, out, *near, grad_out, grad_other, lower, upper, cost=SHORT
+            far_kernel, out, *near, grad_out, grad_other, far, cost=SHORT
         )
         grad_in = call(weave_kernel, shape(128, D_OUT), here, other(there), cost=SHORT)
     with jax.named_scope("rows_yx"):
@@ -268,9 +279,9 @@
         weight_update = pl.pallas_call(
             update_kernel,
             out_shape=shape(256, D_OUT),
-            grid=(4,),
+            grid=(2,),
             in_specs=[VMEM] * 3,
-            out_specs=pl.BlockSpec((256, 512), lambda i: (0, i)),
+            out_specs=pl.BlockSpec((256, 1024), lambda i: (0, i)),
             compiler_params=pltpu.CompilerParams(vmem_limit_bytes=32 << 20),
             cost_estimate=SHORT,
         )(update, basis_other, theirs)

time: 149 us -> 147 us (0.987)
  waiting for transfers between devices: 31.5 us -> 38.2 us
  starting transfers between devices: 74.1 us -> 68.1 us
  local copies, waits for them, and re-layouts: 7.56 us -> 4.04 us
  Pallas kernels: 12.7 us -> 14.4 us
    ppermute x4 -> x2, starting transfers between devices: 11.8 us -> 5.27 us  [shift(): return lax.ppermute(a, 'x', [(i, (i + k) % 4) for i in range(4)])]
    ppermute x0 -> x1, starting transfers between devices: none -> 4.5 us  [on_device(): far = lax.ppermute(passed, ('c', 'x'), onward)]
    all_to_all x5, waiting for transfers between devices: 26.9 us -> 31.2 us  [exchange(): return lax.all_to_all(a, axes, 0, 0, tiled=True)]
    unnamed x36 -> x24, local copies, waits for them, and re-layouts: 7.56 us -> 4.04 us
    ppermute x4, starting transfers between devices: 15.7 us -> 12.7 us  [other(): return lax.ppermute(a, 'c', swap)]
    ppermute x0 -> x1, waiting for transfers between devices: none -> 3.07 us  [on_device(): far = lax.ppermute(passed, ('c', 'x'), onward)]
    pallas_call x13, Pallas kernels: 10.6 us -> 13 us  [call(): pl.pallas_call(body, out_shape=outs, in_specs=specs, out_specs=(VMEM,) *...]
  transfers between devices with their start and end apart: 14 -> 13, of which waited for: 7 -> 9; matrix products, arithmetic and copies ran while one was open for 0% -> 0% of each run, Pallas kernels for 6% -> 8%
where the time goes in v4:
time: 147 us; the launch traced here: 146 us
  starting transfers between devices  68.1 us (46%)
  waiting for transfers between devices  38.2 us (26%)
  blocking collectives  17.9 us (12%)
  Pallas kernels  14.4 us (10%)
  local copies, waits for them, and re-layouts  4.04 us (3%)
  matrix products  2.36 us (2%)
    all_to_all x5, starting transfers between devices, exchange(): return lax.all_to_all(a, axes, 0, 0, tiled=True)  41 us
    all_to_all x5, waiting for transfers between devices, exchange(): return lax.all_to_all(a, axes, 0, 0, tiled=True)  31.2 us
    all_to_all x1, blocking collectives, exchange(): return lax.all_to_all(a, axes, 0, 0, tiled=True)  17.9 us
    pallas_call x13, Pallas kernels, call(): pl.pallas_call(body, out_shape=outs, in_specs=specs, out_specs=(VMEM,) *...  13 us
    ppermute x4, starting transfers between devices, other(): return lax.ppermute(a, 'c', swap)  12.7 us
    ppermute x2, starting transfers between devices, shift(): return lax.ppermute(a, 'x', [(i, (i + k) % 4) for i in range(4)])  5.27 us
    ppermute x1, starting transfers between devices, on_device(): cross = lax.ppermute(half, 'yh', swap)  4.67 us
    ppermute x1, starting transfers between devices, on_device(): far = lax.ppermute(passed, ('c', 'x'), onward)  4.5 us
  transfers between devices with their start and end apart: 13, of which 9 were waited for; matrix products, arithmetic and copies ran while one was open for 0% of the time, Pallas kernels for 8%

profile of v4, /device:TPU:1, one launch (start us, length us, event | category | flops | bytes accessed | tf_op | source)
XLA Modules:
  0.0 145.9 jit_solution(12407032465099198021)
XLA Ops:
  1.6 1.2 pick.1
  2.8 7.6 %all-to-all-start = ((bf16[8,256,256]{2,1,0:T(8,128)(2,1)}), bf16[8,256,256]{2,1,0:T(8,128)(2,1)S(1)}, u32[]{:S(2)}, u32[]{:S(2)}) async-start(bf16[8,256,256]{2,1,0:T(8,128)(2,1)} %get-tuple-element.22), calls=%async_computation | async-start | bytes 2097152 | tf_op jit(solution)/shard_map/basis/all_to_all | solution.py:194
  10.4 4.9 %collective-permute-start = (bf16[128,2048]{1,0:T(8,128)(2,1)S(1)}, bf16[128,2048]{1,0:T(8,128)(2,1)S(1)}, u32[]{:S(2)}, u32[]{:S(2)}) collective-permute-start(bf16[128,2048]{1,0:T(8,128)(2,1)S(1)} %copy-done.11), channel_id=1, source_target_pairs={{0,8},{8,0},{1,9},{9,1},{2,10},{10,2},{3,11},{11,3},{4,12},{12,4},... | collective-permute-start | bytes 1572872 | tf_op jit(solution)/shard_map/swap_tokens/ppermute | solution.py:206
  15.3 1.9 %collective-permute-start.1 = (bf16[128,2048]{1,0:T(8,128)(2,1)S(1)}, bf16[128,2048]{1,0:T(8,128)(2,1)S(1)}, u32[]{:S(2)}, u32[]{:S(2)}) collective-permute-start(bf16[128,2048]{1,0:T(8,128)(2,1)S(1)} %copy-done.1), channel_id=1, source_target_pairs={{0,8},{8,0},{1,9},{9,1},{2,10},{10,2},{3,11},{11,3},{4,12},{12,4},... | collective-permute-start | bytes 1572872 | tf_op jit(solution)/shard_map/swap_tokens/ppermute | solution.py:206
  17.3 1.9 %collective-permute-done.1.other_ref = bf16[128,2048]{1,0:T(8,128)(2,1)S(1)} collective-permute-done((bf16[128,2048]{1,0:T(8,128)(2,1)S(1)}, bf16[128,2048]{1,0:T(8,128)(2,1)S(1)}, u32[]{:S(2)}, u32[]{:S(2)}) %collective-permute-start.1) | collective-permute-done | bytes 524320 | tf_op jit(solution)/shard_map/swap_tokens/ppermute | solution.py:206
  19.1 8.5 %all-to-all-done = bf16[8,256,256]{2,1,0:T(8,128)(2,1)S(1)} async-done(((bf16[8,256,256]{2,1,0:T(8,128)(2,1)}), bf16[8,256,256]{2,1,0:T(8,128)(2,1)S(1)}, u32[]{:S(2)}, u32[]{:S(2)}) %all-to-all-start) | async-done | bytes 1048608 | tf_op jit(solution)/shard_map/basis/all_to_all | solution.py:194
  27.6 2.4 %convolution_convert_fusion._ = bf16[256,2048]{1,0:T(8,128)(2,1)} fusion(bf16[2048,256]{1,0:T(8,128)(2,1)S(1)} %bitcast.18, bf16[128,2048]{1,0:T(8,128)(2,1)S(1)} %collective-permute-done, bf16[128,2048]{1,0:T(8,128)(2,1)S(1)} %copy-done.11, bf16[128,2048]{1,0:T(8,128)(2,1)S(1)} %collective-permute-done.1.other_ref, bf16[128,2048]{1,0:T(8,128)(2,1)S(1)} %copy-done.1), kind=kOutput, calls=%fused_computation | convolution fusion | flops 541655040 | bytes 4194304 | tf_op jit(solution)/shard_map/projected/dot_general | solution.py:220
  30.0 3.8 %all-to-all-start.1 = ((bf16[16,16,2048]{2,1,0:T(8,128)(2,1)}), bf16[16,16,2048]{2,1,0:T(8,128)(2,1)S(1)}, u32[]{:S(2)}, u32[]{:S(2)}) async-start(bf16[16,16,2048]{2,1,0:T(8,128)(2,1)} %bitcast.1), calls=%async_computation.1 | async-start | bytes 2097152 | tf_op jit(solution)/shard_map/sum_yx/all_to_all | solution.py:194
  33.8 4.7 %collective-permute-start.2 = (bf16[128,2048]{1,0:T(8,128)(2,1)S(1)}, bf16[128,2048]{1,0:T(8,128)(2,1)S(1)}, u32[]{:S(2)}, u32[]{:S(2)}) collective-permute-start(bf16[128,2048]{1,0:T(8,128)(2,1)S(1)} %weight_y.1.a_ref), channel_id=1, source_target_pairs={{0,4},{4,0},{1,5},{5,1},{2,6},{6,2},{3,7},{7,3},{8,12},{12,8},{9,1... | collective-permute-start | bytes 1572872 | tf_op jit(solution)/shard_map/weight_y/ppermute | solution.py:226
  38.5 11.8 %all-to-all-done.1.in_ref = bf16[16,16,2048]{2,1,0:T(8,128)(2,1)S(1)} async-done(((bf16[16,16,2048]{2,1,0:T(8,128)(2,1)}), bf16[16,16,2048]{2,1,0:T(8,128)(2,1)S(1)}, u32[]{:S(2)}, u32[]{:S(2)}) %all-to-all-start.1) | async-done | bytes 1048608 | tf_op jit(solution)/shard_map/sum_yx/all_to_all | solution.py:194
  51.2 15.3 %all-to-all-start.2 = ((f32[16,16,128]{2,1,0:T(8,128)}), f32[16,16,128]{2,1,0:T(8,128)S(1)}, u32[]{:S(2)}, u32[]{:S(2)}) async-start(f32[16,16,128]{2,1,0:T(8,128)} %sum_yx.1._), calls=%async_computation.2 | async-start | bytes 262144 | tf_op jit(solution)/shard_map/sum_z/all_to_all | solution.py:194
  66.5 1.1 weight_x.1.pair
  67.6 1.9 %collective-permute-start.4 = (bf16[256,2048]{1,0:T(8,128)(2,1)}, bf16[256,2048]{1,0:T(8,128)(2,1)S(1)}, u32[]{:S(2)}, u32[]{:S(2)}) collective-permute-start(bf16[256,2048]{1,0:T(8,128)(2,1)} %weight_x.1.pair), channel_id=1, source_target_pairs={{0,3},{1,0},{2,1},{3,2},{4,7},{5,4},{6,5},{7,6},{8,11},{9,8},{10,9... | collective-permute-start | bytes 3145736 | tf_op jit(solution)/shard_map/weight_x/ppermute | solution.py:198
  69.5 3.4 %collective-permute-start.3 = (bf16[256,2048]{1,0:T(8,128)(2,1)}, bf16[256,2048]{1,0:T(8,128)(2,1)S(1)}, u32[]{:S(2)}, u32[]{:S(2)}) collective-permute-start(bf16[256,2048]{1,0:T(8,128)(2,1)} %weight_x.1.pair), channel_id=1, source_target_pairs={{0,1},{1,2},{2,3},{3,0},{4,5},{5,6},{6,7},{7,4},{8,9},{9,10},{10,1... | collective-permute-start | bytes 3145736 | tf_op jit(solution)/shard_map/weight_x/ppermute | solution.py:198
  72.8 5.7 %all-to-all-done.2.in_ref = f32[16,16,128]{2,1,0:T(8,128)S(1)} async-done(((f32[16,16,128]{2,1,0:T(8,128)}), f32[16,16,128]{2,1,0:T(8,128)S(1)}, u32[]{:S(2)}, u32[]{:S(2)}) %all-to-all-start.2) | async-done | bytes 131104 | tf_op jit(solution)/shard_map/sum_z/all_to_all | solution.py:194
  78.6 17.9 %all_to_all.37.rows_ref = bf16[16,48,128]{2,1,0:T(8,128)(2,1)S(1)} all-to-all(bf16[16,48,128]{2,1,0:T(8,128)(2,1)S(1)} %get-tuple-element.26), channel_id=1, replica_groups=mesh['yl'=2,'z'=16,'c'=2,'yh'=2,'x'=4] {'z'}, dimensions={0} | all-to-all | bytes 393216 | tf_op jit(solution)/shard_map/rows_z/all_to_all | solution.py:194
  97.3 9.8 %all-to-all-start.4 = ((f32[32,1,128]{2,1,0:T(1,128)}), f32[32,1,128]{2,1,0:T(1,128)S(1)}, u32[]{:S(2)}, u32[]{:S(2)}) async-start(f32[32,1,128]{2,1,0:T(1,128)} %bitcast.5), calls=%async_computation.4 | async-start | bytes 32768 | tf_op jit(solution)/shard_map/total/all_to_all | solution.py:194
  107.2 4.5 %collective-permute-start.5 = (bf16[256,2048]{1,0:T(8,128)(2,1)S(1)}, bf16[256,2048]{1,0:T(8,128)(2,1)}, u32[]{:S(2)}, u32[]{:S(2)}) collective-permute-start(bf16[256,2048]{1,0:T(8,128)(2,1)S(1)} %weight_far.1), channel_id=1, source_target_pairs={{0,1},{1,2},{2,3},{3,0},{8,11},{9,8},{10,9},{11,10},{4,5},{5,6},{6... | collective-permute-start | bytes 3145736 | tf_op jit(solution)/shard_map/weight_far/ppermute | solution.py:253
  111.7 2.3 %all-to-all-done.4 = f32[32,1,128]{2,1,0:T(1,128)S(1)} async-done(((f32[32,1,128]{2,1,0:T(1,128)}), f32[32,1,128]{2,1,0:T(1,128)S(1)}, u32[]{:S(2)}, u32[]{:S(2)}) %all-to-all-start.4) | async-done | bytes 16416 | tf_op jit(solution)/shard_map/total/all_to_all | solution.py:194
  114.0 1.1 adam.1
  116.1 4.5 %all-to-all-start.5 = ((bf16[16,16,2048]{2,1,0:T(8,128)(2,1)}), bf16[16,16,2048]{2,1,0:T(8,128)(2,1)}, u32[]{:S(2)}, u32[]{:S(2)}) async-start(bf16[16,16,2048]{2,1,0:T(8,128)(2,1)} %copy-done), calls=%async_computation.5 | async-start | bytes 2097152 | tf_op jit(solution)/shard_map/rows_yx/all_to_all | solution.py:194
  120.6 1.0 copy-done.2
  121.6 1.0 copy-done.4
  122.6 3.0 %grad_in.3 = (bf16[128,1024]{1,0:T(8,128)(2,1)S(1)}, bf16[128,1024]{1,0:T(8,128)(2,1)S(1)}) custom-call(f32[16,128]{1,0:T(8,128)S(1)} %copy-done.10, bf16[128,2048]{1,0:T(8,128)(2,1)S(1)} %copy-done.2, bf16[128,2048]{1,0:T(8,128)(2,1)S(1)} %copy-done.4, bf16[256,2048]{1,0:T(8,128)(2,1)} %weight_x.1.pair, ...), custom_call_target="tpu_custom_call" | custom-call | flops 20000000000 | bytes 1048576 | tf_op jit(solution)/shard_map/grad_in/pallas_call | solution.py:36
  125.7 3.1 %collective-permute-done.5.far = bf16[256,2048]{1,0:T(8,128)(2,1)} collective-permute-done((bf16[256,2048]{1,0:T(8,128)(2,1)S(1)}, bf16[256,2048]{1,0:T(8,128)(2,1)}, u32[]{:S(2)}, u32[]{:S(2)}) %collective-permute-start.5) | collective-permute-done | bytes 1048608 | tf_op jit(solution)/shard_map/weight_far/ppermute | solution.py:253
  128.7 2.0 %grad_in.4 = (bf16[128,1024]{1,0:T(8,128)(2,1)S(1)}, bf16[128,1024]{1,0:T(8,128)(2,1)S(1)}) custom-call(bf16[128,1024]{1,0:T(8,128)(2,1)S(1)} %get-tuple-element.32.near_here, bf16[128,1024]{1,0:T(8,128)(2,1)S(1)} %get-tuple-element.33.near_there, bf16[128,2048]{1,0:T(8,128)(2,1)S(1)} %copy-done.2, bf16[128,2048]{1,0:T(8,128)(2,1)S(1)} %copy-done.4, ...), custom_call_target="tpu_custom_call" | custom-call | flops 1000 | bytes 1000 | tf_op jit(solution)/shard_map/grad_in/pallas_call | solution.py:36
  130.7 1.9 %collective-permute-start.6 = (bf16[128,1024]{1,0:T(8,128)(2,1)S(1)}, bf16[128,1024]{1,0:T(8,128)(2,1)S(1)}, u32[]{:S(2)}, u32[]{:S(2)}) collective-permute-start(bf16[128,1024]{1,0:T(8,128)(2,1)S(1)} %get-tuple-element.35), channel_id=1, source_target_pairs={{0,8},{8,0},{1,9},{9,1},{2,10},{10,2},{3,11},{11,3},{4,12},{12,4},... | collective-permute-start | bytes 786440 | tf_op jit(solution)/shard_map/grad_in/ppermute | solution.py:206
  132.9 1.2 collective-permute-done.6.there_ref
  135.1 2.9 %all-to-all-done.5 = bf16[16,16,2048]{2,1,0:T(8,128)(2,1)} async-done(((bf16[16,16,2048]{2,1,0:T(8,128)(2,1)}), bf16[16,16,2048]{2,1,0:T(8,128)(2,1)}, u32[]{:S(2)}, u32[]{:S(2)}) %all-to-all-start.5) | async-done | bytes 1048608 | tf_op jit(solution)/shard_map/rows_yx/all_to_all | solution.py:194
  138.0 3.9 %collective-permute-start.7 = (bf16[256,2048]{1,0:T(8,128)(2,1)}, bf16[256,2048]{1,0:T(8,128)(2,1)S(1)}, u32[]{:S(2)}, u32[]{:S(2)}) collective-permute-start(bf16[256,2048]{1,0:T(8,128)(2,1)} %bitcast.7.rows_ref), channel_id=1, source_target_pairs={{0,8},{8,0},{1,9},{9,1},{2,10},{10,2},{3,11},{11,3},{4,12},{12,4},... | collective-permute-start | bytes 3145736 | tf_op jit(solution)/shard_map/update/ppermute | solution.py:206
  142.0 1.7 %update.2.own_ref = f32[256,2048]{1,0:T(8,128)S(1)} custom-call(bf16[256,256]{1,0:T(8,128)(2,1)S(1)} %get-tuple-element.38.basis_ref, bf16[256,2048]{1,0:T(8,128)(2,1)} %bitcast.7.rows_ref), custom_call_target="tpu_custom_call" | custom-call | flops 20000000000 | bytes 1048576 | tf_op jit(solution)/shard_map/update/pallas_call | solution.py:36
  144.4 1.4 update.3
  (34 shorter events, 5.7 us)
Async XLA Ops:
  0.6 1.0 copy-start.6
  2.8 7.6 %copy-start.11 = (bf16[128,2048]{1,0:T(8,128)(2,1)S(1)}, bf16[128,2048]{1,0:T(8,128)(2,1)}, u32[]{:S(2)}) copy-start(bf16[128,2048]{1,0:T(8,128)(2,1)} %param.6) | copy-start | bytes 1572868
  2.8 12.5 %copy-start.1 = (bf16[128,2048]{1,0:T(8,128)(2,1)S(1)}, bf16[128,2048]{1,0:T(8,128)(2,1)}, u32[]{:S(2)}) copy-start(bf16[128,2048]{1,0:T(8,128)(2,1)} %grad_ref.3) | copy-start | bytes 1572868
  2.8 24.8 %all-to-all-start = ((bf16[8,256,256]{2,1,0:T(8,128)(2,1)}), bf16[8,256,256]{2,1,0:T(8,128)(2,1)S(1)}, u32[]{:S(2)}, u32[]{:S(2)}) async-start(bf16[8,256,256]{2,1,0:T(8,128)(2,1)} %get-tuple-element.22), calls=%async_computation | async-start | bytes 2097152 | tf_op jit(solution)/shard_map/basis/all_to_all | solution.py:194
  10.4 6.8 %collective-permute-start = (bf16[128,2048]{1,0:T(8,128)(2,1)S(1)}, bf16[128,2048]{1,0:T(8,128)(2,1)S(1)}, u32[]{:S(2)}, u32[]{:S(2)}) collective-permute-start(bf16[128,2048]{1,0:T(8,128)(2,1)S(1)} %copy-done.11), channel_id=1, source_target_pairs={{0,8},{8,0},{1,9},{9,1},{2,10},{10,2},{3,11},{11,3},{4,12},{12,4},... | collective-permute-start | bytes 1572872 | tf_op jit(solution)/shard_map/swap_tokens/ppermute | solution.py:206
  15.3 3.8 %collective-permute-start.1 = (bf16[128,2048]{1,0:T(8,128)(2,1)S(1)}, bf16[128,2048]{1,0:T(8,128)(2,1)S(1)}, u32[]{:S(2)}, u32[]{:S(2)}) collective-permute-start(bf16[128,2048]{1,0:T(8,128)(2,1)S(1)} %copy-done.1), channel_id=1, source_target_pairs={{0,8},{8,0},{1,9},{9,1},{2,10},{10,2},{3,11},{11,3},{4,12},{12,4},... | collective-permute-start | bytes 1572872 | tf_op jit(solution)/shard_map/swap_tokens/ppermute | solution.py:206
  19.1 10.8 %copy-start.3 = (bf16[128,2048]{1,0:T(8,128)(2,1)}, bf16[128,2048]{1,0:T(8,128)(2,1)S(1)}, u32[]{:S(2)}) copy-start(bf16[128,2048]{1,0:T(8,128)(2,1)S(1)} %collective-permute-done.1.other_ref) | copy-start | bytes 1572868
  30.0 3.8 %copy-start.5 = (bf16[256,2048]{1,0:T(8,128)(2,1)S(1)}, bf16[256,2048]{1,0:T(8,128)(2,1)}, u32[]{:S(2)}) copy-start(bf16[256,2048]{1,0:T(8,128)(2,1)} %w_ref.1) | copy-start | bytes 3145732
  30.0 20.3 %all-to-all-start.1 = ((bf16[16,16,2048]{2,1,0:T(8,128)(2,1)}), bf16[16,16,2048]{2,1,0:T(8,128)(2,1)S(1)}, u32[]{:S(2)}, u32[]{:S(2)}) async-start(bf16[16,16,2048]{2,1,0:T(8,128)(2,1)} %bitcast.1), calls=%async_computation.1 | async-start | bytes 2097152 | tf_op jit(solution)/shard_map/sum_yx/all_to_all | solution.py:194
  33.8 32.7 %collective-permute-start.2 = (bf16[128,2048]{1,0:T(8,128)(2,1)S(1)}, bf16[128,2048]{1,0:T(8,128)(2,1)S(1)}, u32[]{:S(2)}, u32[]{:S(2)}) collective-permute-start(bf16[128,2048]{1,0:T(8,128)(2,1)S(1)} %weight_y.1.a_ref), channel_id=1, source_target_pairs={{0,4},{4,0},{1,5},{5,1},{2,6},{6,2},{3,7},{7,3},{8,12},{12,8},{9,1... | collective-permute-start | bytes 1572872 | tf_op jit(solution)/shard_map/weight_y/ppermute | solution.py:226
  51.2 27.4 %all-to-all-start.2 = ((f32[16,16,128]{2,1,0:T(8,128)}), f32[16,16,128]{2,1,0:T(8,128)S(1)}, u32[]{:S(2)}, u32[]{:S(2)}) async-start(f32[16,16,128]{2,1,0:T(8,128)} %sum_yx.1._), calls=%async_computation.2 | async-start | bytes 262144 | tf_op jit(solution)/shard_map/sum_z/all_to_all | solution.py:194
  66.5 12.1 %copy-start.8 = (f32[1,2048]{1,0:T(1,128)S(1)}, f32[1,2048]{1,0:T(1,128)}, u32[]{:S(2)}) copy-start(f32[1,2048]{1,0:T(1,128)} %param.10) | copy-start | bytes 24580
  66.5 12.1 %copy-start.9 = (f32[1,2048]{1,0:T(1,128)S(1)}, f32[1,2048]{1,0:T(1,128)}, u32[]{:S(2)}) copy-start(f32[1,2048]{1,0:T(1,128)} %param.11) | copy-start | bytes 24580
  67.6 39.5 %collective-permute-start.4 = (bf16[256,2048]{1,0:T(8,128)(2,1)}, bf16[256,2048]{1,0:T(8,128)(2,1)S(1)}, u32[]{:S(2)}, u32[]{:S(2)}) collective-permute-start(bf16[256,2048]{1,0:T(8,128)(2,1)} %weight_x.1.pair), channel_id=1, source_target_pairs={{0,3},{1,0},{2,1},{3,2},{4,7},{5,4},{6,5},{7,6},{8,11},{9,8},{10,9... | collective-permute-start | bytes 3145736 | tf_op jit(solution)/shard_map/weight_x/ppermute | solution.py:198
  69.5 37.6 %collective-permute-start.3 = (bf16[256,2048]{1,0:T(8,128)(2,1)}, bf16[256,2048]{1,0:T(8,128)(2,1)S(1)}, u32[]{:S(2)}, u32[]{:S(2)}) collective-permute-start(bf16[256,2048]{1,0:T(8,128)(2,1)} %weight_x.1.pair), channel_id=1, source_target_pairs={{0,1},{1,2},{2,3},{3,0},{4,5},{5,6},{6,7},{7,4},{8,9},{9,10},{10,1... | collective-permute-start | bytes 3145736 | tf_op jit(solution)/shard_map/weight_x/ppermute | solution.py:198
  97.3 16.7 %all-to-all-start.4 = ((f32[32,1,128]{2,1,0:T(1,128)}), f32[32,1,128]{2,1,0:T(1,128)S(1)}, u32[]{:S(2)}, u32[]{:S(2)}) async-start(f32[32,1,128]{2,1,0:T(1,128)} %bitcast.5), calls=%async_computation.4 | async-start | bytes 32768 | tf_op jit(solution)/shard_map/total/all_to_all | solution.py:194
  107.2 21.6 %collective-permute-start.5 = (bf16[256,2048]{1,0:T(8,128)(2,1)S(1)}, bf16[256,2048]{1,0:T(8,128)(2,1)}, u32[]{:S(2)}, u32[]{:S(2)}) collective-permute-start(bf16[256,2048]{1,0:T(8,128)(2,1)S(1)} %weight_far.1), channel_id=1, source_target_pairs={{0,1},{1,2},{2,3},{3,0},{8,11},{9,8},{10,9},{11,10},{4,5},{5,6},{6... | collective-permute-start | bytes 3145736 | tf_op jit(solution)/shard_map/weight_far/ppermute | solution.py:253
  115.1 1.0 copy-start
  116.1 4.5 %copy-start.10 = (f32[16,128]{1,0:T(8,128)S(1)}, f32[16,128]{1,0:T(8,128)}, u32[]{:S(2)}) copy-start(f32[16,128]{1,0:T(8,128)} %get-tuple-element.30._) | copy-start | bytes 24580
  116.1 22.0 %all-to-all-start.5 = ((bf16[16,16,2048]{2,1,0:T(8,128)(2,1)}), bf16[16,16,2048]{2,1,0:T(8,128)(2,1)}, u32[]{:S(2)}, u32[]{:S(2)}) async-start(bf16[16,16,2048]{2,1,0:T(8,128)(2,1)} %copy-done), calls=%async_computation.5 | async-start | bytes 2097152 | tf_op jit(solution)/shard_map/rows_yx/all_to_all | solution.py:194
  120.6 1.0 copy-start.2
  121.6 1.0 copy-start.4
  125.7 7.0 %copy-start.7 = (bf16[256,512]{1,0:T(8,128)(2,1)S(1)}, bf16[256,512]{1,0:T(8,128)(2,1)}, u32[]{:S(2)}) copy-start(bf16[256,512]{1,0:T(8,128)(2,1)} %basis_ref.3) | copy-start | bytes 786436
  130.7 3.4 %collective-permute-start.6 = (bf16[128,1024]{1,0:T(8,128)(2,1)S(1)}, bf16[128,1024]{1,0:T(8,128)(2,1)S(1)}, u32[]{:S(2)}, u32[]{:S(2)}) collective-permute-start(bf16[128,1024]{1,0:T(8,128)(2,1)S(1)} %get-tuple-element.35), channel_id=1, source_target_pairs={{0,8},{8,0},{1,9},{9,1},{2,10},{10,2},{3,11},{11,3},{4,12},{12,4},... | collective-permute-start | bytes 786440 | tf_op jit(solution)/shard_map/grad_in/ppermute | solution.py:206
  138.0 6.4 %collective-permute-start.7 = (bf16[256,2048]{1,0:T(8,128)(2,1)}, bf16[256,2048]{1,0:T(8,128)(2,1)S(1)}, u32[]{:S(2)}, u32[]{:S(2)}) collective-permute-start(bf16[256,2048]{1,0:T(8,128)(2,1)} %bitcast.7.rows_ref), channel_id=1, source_target_pairs={{0,8},{8,0},{1,9},{9,1},{2,10},{10,2},{3,11},{11,3},{4,12},{12,4},... | collective-permute-start | bytes 3145736 | tf_op jit(solution)/shard_map/update/ppermute | solution.py:206

commit v5 on v4

--- a/solution.py
+++ b/solution.py
@@ -80,6 +80,21 @@
     out_ref[...] = (0.25 * update).astype(bf16)
 
 
+def projected_kernel(acts_ref, acts2_ref, grad_ref, grad2_ref, basis_ref, out_ref):
+    basis = basis_ref[...]
+    coords = [
+        jnp.dot(a[...], basis, preferred_element_type=f32).T.astype(bf16)
+        for a in (acts_ref, acts2_ref)
+    ]
+    for k in range(4):
+        at = pl.ds(k * 512, 512)
+        part = [
+            jnp.dot(c, g[:, at], preferred_element_type=f32)
+            for c, g in zip(coords, (grad_ref, grad2_ref), strict=True)
+        ]
+        out_ref[:, at] = (part[0] + part[1]).astype(bf16)
+
+
 def half_kernel(_, w_ref, o_ref):
     start = pl.multiple_of(lax.axis_index("c") * 128, 128)
     o_ref[...] = w_ref[pl.ds(start, 128)]
@@ -211,15 +226,15 @@
         )
     with jax.named_scope("swap_tokens"):
         grad_other = other(grad_out)
-        acts2 = jnp.concatenate([acts, other(acts)], 0)
-        grad2 = jnp.concatenate([grad_out, grad_other], 0)
+        acts_other = other(acts)
     with jax.named_scope("basis"):
         basis_all = exchange(basis_sent, FSDP).reshape(2048, 256)
     with jax.named_scope("projected"):
-        coords = jnp.dot(acts2, basis_all, preferred_element_type=f32).astype(bf16)
-        part = lax.dot_general(
-            coords, grad2, (((0,), (0,)), ((), ())), preferred_element_type=f32
-        ).astype(bf16)
+        part = call(
+            projected_kernel,
+            shape(256, D_OUT),
+            acts, acts_other, grad_out, grad_other, basis_all,
+        )
         basis_other = call(pick_other_kernel, shape(256, 256), basis, first=part)
     with jax.named_scope("weight_y"):
         half = call(half_kernel, shape(128, 2048), weight, first=part)

time: 147 us -> 147 us (level)
  matrix products: 2.36 us -> 0 us
  Pallas kernels: 14.4 us -> 16.6 us
    dot_general x1 -> x0, matrix products: 2.36 us -> none  [on_device(): lax.dot_general(coords, grad2, (((0,), (0,)), ((), ())), preferred_elemen...]
    pallas_call x13 -> x14, Pallas kernels: 13 us -> 15.1 us  [call(): pl.pallas_call(body, out_shape=outs, in_specs=specs, out_specs=(VMEM,) *...]
where the time goes in v5:
time: 147 us; the launch traced here: 146 us
  starting transfers between devices  68.1 us (46%)
  waiting for transfers between devices  38.2 us (26%)
  blocking collectives  17.9 us (12%)
  Pallas kernels  16.6 us (11%)
  local copies, waits for them, and re-layouts  4.04 us (3%)
    all_to_all x5, starting transfers between devices, exchange(): return lax.all_to_all(a, axes, 0, 0, tiled=True)  41 us
    all_to_all x5, waiting for transfers between devices, exchange(): return lax.all_to_all(a, axes, 0, 0, tiled=True)  31.2 us
    all_to_all x1, blocking collectives, exchange(): return lax.all_to_all(a, axes, 0, 0, tiled=True)  17.9 us
    pallas_call x14, Pallas kernels, call(): pl.pallas_call(body, out_shape=outs, in_specs=specs, out_specs=(VMEM,) *...  15.1 us
    ppermute x4, starting transfers between devices, other(): return lax.ppermute(a, 'c', swap)  12.7 us
    ppermute x2, starting transfers between devices, shift(): return lax.ppermute(a, 'x', [(i, (i + k) % 4) for i in range(4)])  5.27 us
    ppermute x1, starting transfers between devices, on_device(): cross = lax.ppermute(half, 'yh', swap)  4.67 us
    ppermute x1, starting transfers between devices, on_device(): far = lax.ppermute(passed, ('c', 'x'), onward)  4.5 us
  transfers between devices with their start and end apart: 13, of which 9 were waited for; matrix products, arithmetic and copies ran while one was open for 0% of the time, Pallas kernels for 8%

profile of v5, /device:TPU:1, one launch (start us, length us, event | category | flops | bytes accessed | tf_op | source)
XLA Modules:
  0.0 145.6 jit_solution(18064627044359833494)
XLA Ops:
  1.6 1.2 pick.1
  2.8 7.6 %all-to-all-start = ((bf16[8,256,256]{2,1,0:T(8,128)(2,1)}), bf16[8,256,256]{2,1,0:T(8,128)(2,1)S(1)}, u32[]{:S(2)}, u32[]{:S(2)}) async-start(bf16[8,256,256]{2,1,0:T(8,128)(2,1)} %get-tuple-element.22), calls=%async_computation | async-start | bytes 2097152 | tf_op jit(solution)/shard_map/basis/all_to_all | solution.py:209
  10.4 4.9 %collective-permute-start = (bf16[128,2048]{1,0:T(8,128)(2,1)S(1)}, bf16[128,2048]{1,0:T(8,128)(2,1)S(1)}, u32[]{:S(2)}, u32[]{:S(2)}) collective-permute-start(bf16[128,2048]{1,0:T(8,128)(2,1)S(1)} %copy-done.6), channel_id=1, source_target_pairs={{0,8},{8,0},{1,9},{9,1},{2,10},{10,2},{3,11},{11,3},{4,12},{12,4},... | collective-permute-start | bytes 1572872 | tf_op jit(solution)/shard_map/swap_tokens/ppermute | solution.py:221
  15.3 1.9 %collective-permute-start.1 = (bf16[128,2048]{1,0:T(8,128)(2,1)S(1)}, bf16[128,2048]{1,0:T(8,128)(2,1)S(1)}, u32[]{:S(2)}, u32[]{:S(2)}) collective-permute-start(bf16[128,2048]{1,0:T(8,128)(2,1)S(1)} %copy-done.1), channel_id=1, source_target_pairs={{0,8},{8,0},{1,9},{9,1},{2,10},{10,2},{3,11},{11,3},{4,12},{12,4},... | collective-permute-start | bytes 1572872 | tf_op jit(solution)/shard_map/swap_tokens/ppermute | solution.py:221
  17.3 1.9 %collective-permute-done.1.grad2_ref.other_ref = bf16[128,2048]{1,0:T(8,128)(2,1)S(1)} collective-permute-done((bf16[128,2048]{1,0:T(8,128)(2,1)S(1)}, bf16[128,2048]{1,0:T(8,128)(2,1)S(1)}, u32[]{:S(2)}, u32[]{:S(2)}) %collective-permute-start.1) | collective-permute-done | bytes 524320 | tf_op jit(solution)/shard_map/swap_tokens/ppermute | solution.py:221
  19.1 8.5 %all-to-all-done = bf16[8,256,256]{2,1,0:T(8,128)(2,1)S(1)} async-done(((bf16[8,256,256]{2,1,0:T(8,128)(2,1)}), bf16[8,256,256]{2,1,0:T(8,128)(2,1)S(1)}, u32[]{:S(2)}, u32[]{:S(2)}) %all-to-all-start) | async-done | bytes 1048608 | tf_op jit(solution)/shard_map/basis/all_to_all | solution.py:209
  27.6 2.1 %projected.2._ = bf16[256,2048]{1,0:T(8,128)(2,1)} custom-call(bf16[128,2048]{1,0:T(8,128)(2,1)S(1)} %copy-done.6, bf16[128,2048]{1,0:T(8,128)(2,1)S(1)} %collective-permute-done.acts2_ref, bf16[128,2048]{1,0:T(8,128)(2,1)S(1)} %copy-done.1, bf16[128,2048]{1,0:T(8,128)(2,1)S(1)} %collective-permute-done.1.grad2_ref.other_ref, bf16[2048,256]{1,0:T(8,128)(2,1)S(1)} %bitcast.11), custom_call_target="tpu_custom_call" | custom-call | flops 20000000000 | bytes 1048576 | tf_op jit(solution)/shard_map/projected/pallas_call | solution.py:36
  29.8 3.8 %all-to-all-start.1 = ((bf16[16,16,2048]{2,1,0:T(8,128)(2,1)}), bf16[16,16,2048]{2,1,0:T(8,128)(2,1)S(1)}, u32[]{:S(2)}, u32[]{:S(2)}) async-start(bf16[16,16,2048]{2,1,0:T(8,128)(2,1)} %bitcast.1), calls=%async_computation.1 | async-start | bytes 2097152 | tf_op jit(solution)/shard_map/sum_yx/all_to_all | solution.py:209
  33.6 4.7 %collective-permute-start.2 = (bf16[128,2048]{1,0:T(8,128)(2,1)S(1)}, bf16[128,2048]{1,0:T(8,128)(2,1)S(1)}, u32[]{:S(2)}, u32[]{:S(2)}) collective-permute-start(bf16[128,2048]{1,0:T(8,128)(2,1)S(1)} %weight_y.1.a_ref), channel_id=1, source_target_pairs={{0,4},{4,0},{1,5},{5,1},{2,6},{6,2},{3,7},{7,3},{8,12},{12,8},{9,1... | collective-permute-start | bytes 1572872 | tf_op jit(solution)/shard_map/weight_y/ppermute | solution.py:241
  38.3 11.8 %all-to-all-done.1.in_ref = bf16[16,16,2048]{2,1,0:T(8,128)(2,1)S(1)} async-done(((bf16[16,16,2048]{2,1,0:T(8,128)(2,1)}), bf16[16,16,2048]{2,1,0:T(8,128)(2,1)S(1)}, u32[]{:S(2)}, u32[]{:S(2)}) %all-to-all-start.1) | async-done | bytes 1048608 | tf_op jit(solution)/shard_map/sum_yx/all_to_all | solution.py:209
  51.0 15.3 %all-to-all-start.2 = ((f32[16,16,128]{2,1,0:T(8,128)}), f32[16,16,128]{2,1,0:T(8,128)S(1)}, u32[]{:S(2)}, u32[]{:S(2)}) async-start(f32[16,16,128]{2,1,0:T(8,128)} %sum_yx.1._), calls=%async_computation.2 | async-start | bytes 262144 | tf_op jit(solution)/shard_map/sum_z/all_to_all | solution.py:209
  66.3 1.1 weight_x.1.pair
  67.3 1.9 %collective-permute-start.4 = (bf16[256,2048]{1,0:T(8,128)(2,1)}, bf16[256,2048]{1,0:T(8,128)(2,1)S(1)}, u32[]{:S(2)}, u32[]{:S(2)}) collective-permute-start(bf16[256,2048]{1,0:T(8,128)(2,1)} %weight_x.1.pair), channel_id=1, source_target_pairs={{0,3},{1,0},{2,1},{3,2},{4,7},{5,4},{6,5},{7,6},{8,11},{9,8},{10,9... | collective-permute-start | bytes 3145736 | tf_op jit(solution)/shard_map/weight_x/ppermute | solution.py:213
  69.3 3.4 %collective-permute-start.3 = (bf16[256,2048]{1,0:T(8,128)(2,1)}, bf16[256,2048]{1,0:T(8,128)(2,1)S(1)}, u32[]{:S(2)}, u32[]{:S(2)}) collective-permute-start(bf16[256,2048]{1,0:T(8,128)(2,1)} %weight_x.1.pair), channel_id=1, source_target_pairs={{0,1},{1,2},{2,3},{3,0},{4,5},{5,6},{6,7},{7,4},{8,9},{9,10},{10,1... | collective-permute-start | bytes 3145736 | tf_op jit(solution)/shard_map/weight_x/ppermute | solution.py:213
  72.6 5.7 %all-to-all-done.2.in_ref = f32[16,16,128]{2,1,0:T(8,128)S(1)} async-done(((f32[16,16,128]{2,1,0:T(8,128)}), f32[16,16,128]{2,1,0:T(8,128)S(1)}, u32[]{:S(2)}, u32[]{:S(2)}) %all-to-all-start.2) | async-done | bytes 131104 | tf_op jit(solution)/shard_map/sum_z/all_to_all | solution.py:209
  78.4 17.9 %all_to_all.37.rows_ref = bf16[16,48,128]{2,1,0:T(8,128)(2,1)S(1)} all-to-all(bf16[16,48,128]{2,1,0:T(8,128)(2,1)S(1)} %get-tuple-element.26), channel_id=1, replica_groups=mesh['yl'=2,'z'=16,'c'=2,'yh'=2,'x'=4] {'z'}, dimensions={0} | all-to-all | bytes 393216 | tf_op jit(solution)/shard_map/rows_z/all_to_all | solution.py:209
  97.0 9.8 %all-to-all-start.4 = ((f32[32,1,128]{2,1,0:T(1,128)}), f32[32,1,128]{2,1,0:T(1,128)S(1)}, u32[]{:S(2)}, u32[]{:S(2)}) async-start(f32[32,1,128]{2,1,0:T(1,128)} %bitcast.5), calls=%async_computation.4 | async-start | bytes 32768 | tf_op jit(solution)/shard_map/total/all_to_all | solution.py:209
  107.0 4.5 %collective-permute-start.5 = (bf16[256,2048]{1,0:T(8,128)(2,1)S(1)}, bf16[256,2048]{1,0:T(8,128)(2,1)}, u32[]{:S(2)}, u32[]{:S(2)}) collective-permute-start(bf16[256,2048]{1,0:T(8,128)(2,1)S(1)} %weight_far.1), channel_id=1, source_target_pairs={{0,1},{1,2},{2,3},{3,0},{8,11},{9,8},{10,9},{11,10},{4,5},{5,6},{6... | collective-permute-start | bytes 3145736 | tf_op jit(solution)/shard_map/weight_far/ppermute | solution.py:268
  111.5 2.3 %all-to-all-done.4 = f32[32,1,128]{2,1,0:T(1,128)S(1)} async-done(((f32[32,1,128]{2,1,0:T(1,128)}), f32[32,1,128]{2,1,0:T(1,128)S(1)}, u32[]{:S(2)}, u32[]{:S(2)}) %all-to-all-start.4) | async-done | bytes 16416 | tf_op jit(solution)/shard_map/total/all_to_all | solution.py:209
  113.7 1.1 adam.1
  115.8 4.5 %all-to-all-start.5 = ((bf16[16,16,2048]{2,1,0:T(8,128)(2,1)}), bf16[16,16,2048]{2,1,0:T(8,128)(2,1)}, u32[]{:S(2)}, u32[]{:S(2)}) async-start(bf16[16,16,2048]{2,1,0:T(8,128)(2,1)} %copy-done), calls=%async_computation.5 | async-start | bytes 2097152 | tf_op jit(solution)/shard_map/rows_yx/all_to_all | solution.py:209
  120.3 1.0 copy-done.2
  121.4 1.0 copy-done.4
  122.4 3.0 %grad_in.3 = (bf16[128,1024]{1,0:T(8,128)(2,1)S(1)}, bf16[128,1024]{1,0:T(8,128)(2,1)S(1)}) custom-call(f32[16,128]{1,0:T(8,128)S(1)} %copy-done.11, bf16[128,2048]{1,0:T(8,128)(2,1)S(1)} %copy-done.2, bf16[128,2048]{1,0:T(8,128)(2,1)S(1)} %copy-done.4, bf16[256,2048]{1,0:T(8,128)(2,1)} %weight_x.1.pair, ...), custom_call_target="tpu_custom_call" | custom-call | flops 20000000000 | bytes 1048576 | tf_op jit(solution)/shard_map/grad_in/pallas_call | solution.py:36
  125.5 3.1 %collective-permute-done.5.far = bf16[256,2048]{1,0:T(8,128)(2,1)} collective-permute-done((bf16[256,2048]{1,0:T(8,128)(2,1)S(1)}, bf16[256,2048]{1,0:T(8,128)(2,1)}, u32[]{:S(2)}, u32[]{:S(2)}) %collective-permute-start.5) | collective-permute-done | bytes 1048608 | tf_op jit(solution)/shard_map/weight_far/ppermute | solution.py:268
  128.5 2.0 %grad_in.4 = (bf16[128,1024]{1,0:T(8,128)(2,1)S(1)}, bf16[128,1024]{1,0:T(8,128)(2,1)S(1)}) custom-call(bf16[128,1024]{1,0:T(8,128)(2,1)S(1)} %get-tuple-element.32.near_here, bf16[128,1024]{1,0:T(8,128)(2,1)S(1)} %get-tuple-element.33.near_there, bf16[128,2048]{1,0:T(8,128)(2,1)S(1)} %copy-done.2, bf16[128,2048]{1,0:T(8,128)(2,1)S(1)} %copy-done.4, ...), custom_call_target="tpu_custom_call" | custom-call | flops 1000 | bytes 1000 | tf_op jit(solution)/shard_map/grad_in/pallas_call | solution.py:36
  130.5 1.9 %collective-permute-start.6 = (bf16[128,1024]{1,0:T(8,128)(2,1)S(1)}, bf16[128,1024]{1,0:T(8,128)(2,1)S(1)}, u32[]{:S(2)}, u32[]{:S(2)}) collective-permute-start(bf16[128,1024]{1,0:T(8,128)(2,1)S(1)} %get-tuple-element.35), channel_id=1, source_target_pairs={{0,8},{8,0},{1,9},{9,1},{2,10},{10,2},{3,11},{11,3},{4,12},{12,4},... | collective-permute-start | bytes 786440 | tf_op jit(solution)/shard_map/grad_in/ppermute | solution.py:221
  132.7 1.2 collective-permute-done.6.there_ref
  134.9 2.9 %all-to-all-done.5 = bf16[16,16,2048]{2,1,0:T(8,128)(2,1)} async-done(((bf16[16,16,2048]{2,1,0:T(8,128)(2,1)}), bf16[16,16,2048]{2,1,0:T(8,128)(2,1)}, u32[]{:S(2)}, u32[]{:S(2)}) %all-to-all-start.5) | async-done | bytes 1048608 | tf_op jit(solution)/shard_map/rows_yx/all_to_all | solution.py:209
  137.8 3.9 %collective-permute-start.7 = (bf16[256,2048]{1,0:T(8,128)(2,1)}, bf16[256,2048]{1,0:T(8,128)(2,1)S(1)}, u32[]{:S(2)}, u32[]{:S(2)}) collective-permute-start(bf16[256,2048]{1,0:T(8,128)(2,1)} %bitcast.7.rows_ref), channel_id=1, source_target_pairs={{0,8},{8,0},{1,9},{9,1},{2,10},{10,2},{3,11},{11,3},{4,12},{12,4},... | collective-permute-start | bytes 3145736 | tf_op jit(solution)/shard_map/update/ppermute | solution.py:221
  141.8 1.7 %update.2.own_ref = f32[256,2048]{1,0:T(8,128)S(1)} custom-call(bf16[256,256]{1,0:T(8,128)(2,1)S(1)} %get-tuple-element.38.basis_ref, bf16[256,2048]{1,0:T(8,128)(2,1)} %bitcast.7.rows_ref), custom_call_target="tpu_custom_call" | custom-call | flops 20000000000 | bytes 1048576 | tf_op jit(solution)/shard_map/update/pallas_call | solution.py:36
  144.2 1.4 update.3
  (34 shorter events, 5.7 us)
Async XLA Ops:
  0.6 1.0 copy-start.7
  2.8 7.6 %copy-start.6 = (bf16[128,2048]{1,0:T(8,128)(2,1)S(1)}, bf16[128,2048]{1,0:T(8,128)(2,1)}, u32[]{:S(2)}) copy-start(bf16[128,2048]{1,0:T(8,128)(2,1)} %acts_ref.1) | copy-start | bytes 1572868
  2.8 12.5 %copy-start.1 = (bf16[128,2048]{1,0:T(8,128)(2,1)S(1)}, bf16[128,2048]{1,0:T(8,128)(2,1)}, u32[]{:S(2)}) copy-start(bf16[128,2048]{1,0:T(8,128)(2,1)} %grad_ref.5) | copy-start | bytes 1572868
  2.8 24.8 %all-to-all-start = ((bf16[8,256,256]{2,1,0:T(8,128)(2,1)}), bf16[8,256,256]{2,1,0:T(8,128)(2,1)S(1)}, u32[]{:S(2)}, u32[]{:S(2)}) async-start(bf16[8,256,256]{2,1,0:T(8,128)(2,1)} %get-tuple-element.22), calls=%async_computation | async-start | bytes 2097152 | tf_op jit(solution)/shard_map/basis/all_to_all | solution.py:209
  10.4 6.8 %collective-permute-start = (bf16[128,2048]{1,0:T(8,128)(2,1)S(1)}, bf16[128,2048]{1,0:T(8,128)(2,1)S(1)}, u32[]{:S(2)}, u32[]{:S(2)}) collective-permute-start(bf16[128,2048]{1,0:T(8,128)(2,1)S(1)} %copy-done.6), channel_id=1, source_target_pairs={{0,8},{8,0},{1,9},{9,1},{2,10},{10,2},{3,11},{11,3},{4,12},{12,4},... | collective-permute-start | bytes 1572872 | tf_op jit(solution)/shard_map/swap_tokens/ppermute | solution.py:221
  15.3 3.8 %collective-permute-start.1 = (bf16[128,2048]{1,0:T(8,128)(2,1)S(1)}, bf16[128,2048]{1,0:T(8,128)(2,1)S(1)}, u32[]{:S(2)}, u32[]{:S(2)}) collective-permute-start(bf16[128,2048]{1,0:T(8,128)(2,1)S(1)} %copy-done.1), channel_id=1, source_target_pairs={{0,8},{8,0},{1,9},{9,1},{2,10},{10,2},{3,11},{11,3},{4,12},{12,4},... | collective-permute-start | bytes 1572872 | tf_op jit(solution)/shard_map/swap_tokens/ppermute | solution.py:221
  19.1 10.6 %copy-start.3 = (bf16[128,2048]{1,0:T(8,128)(2,1)}, bf16[128,2048]{1,0:T(8,128)(2,1)S(1)}, u32[]{:S(2)}) copy-start(bf16[128,2048]{1,0:T(8,128)(2,1)S(1)} %collective-permute-done.1.grad2_ref.other_ref) | copy-start | bytes 1572868
  29.8 3.8 %copy-start.5 = (bf16[256,2048]{1,0:T(8,128)(2,1)S(1)}, bf16[256,2048]{1,0:T(8,128)(2,1)}, u32[]{:S(2)}) copy-start(bf16[256,2048]{1,0:T(8,128)(2,1)} %w_ref.1) | copy-start | bytes 3145732
  29.8 20.3 %all-to-all-start.1 = ((bf16[16,16,2048]{2,1,0:T(8,128)(2,1)}), bf16[16,16,2048]{2,1,0:T(8,128)(2,1)S(1)}, u32[]{:S(2)}, u32[]{:S(2)}) async-start(bf16[16,16,2048]{2,1,0:T(8,128)(2,1)} %bitcast.1), calls=%async_computation.1 | async-start | bytes 2097152 | tf_op jit(solution)/shard_map/sum_yx/all_to_all | solution.py:209
  33.6 32.7 %collective-permute-start.2 = (bf16[128,2048]{1,0:T(8,128)(2,1)S(1)}, bf16[128,2048]{1,0:T(8,128)(2,1)S(1)}, u32[]{:S(2)}, u32[]{:S(2)}) collective-permute-start(bf16[128,2048]{1,0:T(8,128)(2,1)S(1)} %weight_y.1.a_ref), channel_id=1, source_target_pairs={{0,4},{4,0},{1,5},{5,1},{2,6},{6,2},{3,7},{7,3},{8,12},{12,8},{9,1... | collective-permute-start | bytes 1572872 | tf_op jit(solution)/shard_map/weight_y/ppermute | solution.py:241
  51.0 27.4 %all-to-all-start.2 = ((f32[16,16,128]{2,1,0:T(8,128)}), f32[16,16,128]{2,1,0:T(8,128)S(1)}, u32[]{:S(2)}, u32[]{:S(2)}) async-start(f32[16,16,128]{2,1,0:T(8,128)} %sum_yx.1._), calls=%async_computation.2 | async-start | bytes 262144 | tf_op jit(solution)/shard_map/sum_z/all_to_all | solution.py:209
  66.3 12.1 %copy-start.9 = (f32[1,2048]{1,0:T(1,128)S(1)}, f32[1,2048]{1,0:T(1,128)}, u32[]{:S(2)}) copy-start(f32[1,2048]{1,0:T(1,128)} %param.10) | copy-start | bytes 24580
  66.3 12.1 %copy-start.10 = (f32[1,2048]{1,0:T(1,128)S(1)}, f32[1,2048]{1,0:T(1,128)}, u32[]{:S(2)}) copy-start(f32[1,2048]{1,0:T(1,128)} %param.11) | copy-start | bytes 24580
  67.3 39.5 %collective-permute-start.4 = (bf16[256,2048]{1,0:T(8,128)(2,1)}, bf16[256,2048]{1,0:T(8,128)(2,1)S(1)}, u32[]{:S(2)}, u32[]{:S(2)}) collective-permute-start(bf16[256,2048]{1,0:T(8,128)(2,1)} %weight_x.1.pair), channel_id=1, source_target_pairs={{0,3},{1,0},{2,1},{3,2},{4,7},{5,4},{6,5},{7,6},{8,11},{9,8},{10,9... | collective-permute-start | bytes 3145736 | tf_op jit(solution)/shard_map/weight_x/ppermute | solution.py:213
  69.3 37.6 %collective-permute-start.3 = (bf16[256,2048]{1,0:T(8,128)(2,1)}, bf16[256,2048]{1,0:T(8,128)(2,1)S(1)}, u32[]{:S(2)}, u32[]{:S(2)}) collective-permute-start(bf16[256,2048]{1,0:T(8,128)(2,1)} %weight_x.1.pair), channel_id=1, source_target_pairs={{0,1},{1,2},{2,3},{3,0},{4,5},{5,6},{6,7},{7,4},{8,9},{9,10},{10,1... | collective-permute-start | bytes 3145736 | tf_op jit(solution)/shard_map/weight_x/ppermute | solution.py:213
  97.0 16.7 %all-to-all-start.4 = ((f32[32,1,128]{2,1,0:T(1,128)}), f32[32,1,128]{2,1,0:T(1,128)S(1)}, u32[]{:S(2)}, u32[]{:S(2)}) async-start(f32[32,1,128]{2,1,0:T(1,128)} %bitcast.5), calls=%async_computation.4 | async-start | bytes 32768 | tf_op jit(solution)/shard_map/total/all_to_all | solution.py:209
  107.0 21.6 %collective-permute-start.5 = (bf16[256,2048]{1,0:T(8,128)(2,1)S(1)}, bf16[256,2048]{1,0:T(8,128)(2,1)}, u32[]{:S(2)}, u32[]{:S(2)}) collective-permute-start(bf16[256,2048]{1,0:T(8,128)(2,1)S(1)} %weight_far.1), channel_id=1, source_target_pairs={{0,1},{1,2},{2,3},{3,0},{8,11},{9,8},{10,9},{11,10},{4,5},{5,6},{6... | collective-permute-start | bytes 3145736 | tf_op jit(solution)/shard_map/weight_far/ppermute | solution.py:268
  114.9 1.0 copy-start
  115.8 4.5 %copy-start.11 = (f32[16,128]{1,0:T(8,128)S(1)}, f32[16,128]{1,0:T(8,128)}, u32[]{:S(2)}) copy-start(f32[16,128]{1,0:T(8,128)} %get-tuple-element.30._) | copy-start | bytes 24580
  115.8 22.0 %all-to-all-start.5 = ((bf16[16,16,2048]{2,1,0:T(8,128)(2,1)}), bf16[16,16,2048]{2,1,0:T(8,128)(2,1)}, u32[]{:S(2)}, u32[]{:S(2)}) async-start(bf16[16,16,2048]{2,1,0:T(8,128)(2,1)} %copy-done), calls=%async_computation.5 | async-start | bytes 2097152 | tf_op jit(solution)/shard_map/rows_yx/all_to_all | solution.py:209
  120.3 1.0 copy-start.2
  121.4 1.0 copy-start.4
  125.5 7.0 %copy-start.8 = (bf16[256,512]{1,0:T(8,128)(2,1)S(1)}, bf16[256,512]{1,0:T(8,128)(2,1)}, u32[]{:S(2)}) copy-start(bf16[256,512]{1,0:T(8,128)(2,1)} %basis_ref.3) | copy-start | bytes 786436
  130.5 3.4 %collective-permute-start.6 = (bf16[128,1024]{1,0:T(8,128)(2,1)S(1)}, bf16[128,1024]{1,0:T(8,128)(2,1)S(1)}, u32[]{:S(2)}, u32[]{:S(2)}) collective-permute-start(bf16[128,1024]{1,0:T(8,128)(2,1)S(1)} %get-tuple-element.35), channel_id=1, source_target_pairs={{0,8},{8,0},{1,9},{9,1},{2,10},{10,2},{3,11},{11,3},{4,12},{12,4},... | collective-permute-start | bytes 786440 | tf_op jit(solution)/shard_map/grad_in/ppermute | solution.py:221
  137.8 6.4 %collective-permute-start.7 = (bf16[256,2048]{1,0:T(8,128)(2,1)}, bf16[256,2048]{1,0:T(8,128)(2,1)S(1)}, u32[]{:S(2)}, u32[]{:S(2)}) collective-permute-start(bf16[256,2048]{1,0:T(8,128)(2,1)} %bitcast.7.rows_ref), channel_id=1, source_target_pairs={{0,8},{8,0},{1,9},{9,1},{2,10},{10,2},{3,11},{11,3},{4,12},{12,4},... | collective-permute-start | bytes 3145736 | tf_op jit(solution)/shard_map/update/ppermute | solution.py:221
